TPU v7x, 128 devices: a whole 4x4x4 slice. The times are simulated.
128 devices in a mesh: grp: 2 (over x_lo), px: 8 (over x_hi, y), py: 8 (over z, core).
Axes of the slice: x: 4 (x_hi: 2, x_lo: 2; x = x_hi * 2 + x_lo), y: 4, z: 4, core: 2. Of those that a mesh axis runs over, the one named last changes fastest.
Arguments:
- multiplier: float32 [3, 32, 16, 256, 256], P(None, 'py', None, ('grp', 'px')), may hold values from -6 to 6
- auxiliary: float32 [3, 32, 16, 256, 256], P(None, 'py', None, ('grp', 'px')), may hold values from -6 to 6
- density_start: float32 [16, 256, 256], P(None, ('grp', 'px')), may hold values from 0.5 to 2
- density_end: float32 [16, 256, 256], P(None, ('grp', 'px')), may hold values from 0.5 to 2
Outputs:
- multiplier_next: float32 [3, 32, 16, 256, 256], P(None, 'py', None, ('grp', 'px'))
- auxiliary_next: float32 [3, 32, 16, 256, 256], P(None, 'py', None, ('grp', 'px'))
All inputs are finite; a program needn't handle non-finite values.
Results may differ from a plain program's by a relative error of at most 0.0003.
Values sent between devices are 32-bit elements; how exact they have to be, the bound alone decides.
No kernel may reach another device: no remote copies, remote signals or barrier semaphores. Data moves between devices by JAX's collectives and lax.ppermute only.
A program may use at most 64 MiB of HBM per device.

v0:
```python
import functools
import math

import jax
import jax.numpy as jnp
import numpy as np
from jax import lax
from jax.experimental import pallas as pl
from jax.experimental.pallas import tpu as pltpu
from jax.sharding import PartitionSpec as P

NEWTON = 4
ROWS = ("grp", "px")
EVERY = ("grp", "px", "py")
VMEM_BYTES = 48 * 1024 * 1024


def moved(value, axis, steps, wrap):
    count = lax.axis_size(axis)
    pairs = [(i, (i + steps) % count) for i in range(count) if wrap or 0 <= i + steps < count]
    return lax.ppermute(value, axis, pairs)


def hartley_table(length):
    index = np.arange(length)
    angles = (index[:, None] * index[None, :] % length) * (2.0 * np.pi / length)
    return ((np.cos(angles) + np.sin(angles)) / np.sqrt(length)).astype(np.float32)


def halves(value):
    high = value.astype(jnp.bfloat16)
    return high, (value - high.astype(jnp.float32)).astype(jnp.bfloat16)


def table_halves(length):
    table = hartley_table(length)
    high = table.astype(jnp.bfloat16)
    return np.stack([high, (table - high.astype(np.float32)).astype(jnp.bfloat16)])


def elimination_table(levels, row_count, col_count, blocks):
    col = 4.0 * np.sin(np.pi * np.arange(col_count) / col_count) ** 2
    row = 4.0 * np.sin(np.pi * np.arange(row_count) / row_count) ** 2
    eigen = col[:, None] + row[None, :]
    factors = [1.0 / (1.0 + eigen)]
    for _ in range(levels // 2 - 1):
        factors.append(1.0 / (2.0 + eigen - factors[-1]))
    gap = 1.0 - factors[-1] ** 2
    middle = np.where(eigen > 0.0, 1.0 / np.where(eigen > 0.0, gap, 1.0), 0.0)
    table = np.stack(factors + [middle]).astype(np.float32)
    table = table.reshape(levels // 2 + 1, blocks, col_count // blocks, row_count)
    return np.ascontiguousarray(table.transpose(1, 0, 2, 3))


def dot3(left, right, dims):
    (lh, ll), (rh, rl) = left, right
    one = functools.partial(
        lax.dot_general, dimension_numbers=(dims, ((), ())), preferred_element_type=jnp.float32
    )
    return one(lh, rh) + (one(lh, rl) + one(ll, rh))


def exchange_pieces(blocks, width):
    count = len(blocks)
    lanes = count * width
    group = lax.broadcasted_iota(jnp.int32, blocks[0].shape, 1) // width
    step = 1
    while step < count:
        upper = (group // step) % 2 == 1
        fresh = list(blocks)
        for j in range(count):
            if (j // step) % 2 == 0:
                low, high = blocks[j], blocks[j + step]
                fresh[j] = jnp.where(upper, pltpu.roll(high, step * width, 1), low)
                fresh[j + step] = jnp.where(upper, high, pltpu.roll(low, lanes - step * width, 1))
        blocks = fresh
        step *= 2
    return blocks


def source_kernel(
    levels, mult_ref, aux_ref, start_ref, end_ref, before_ref, rim_ref, hart_ref, out_ref
):
    here, pair, rows, cols = mult_ref.shape[1:]
    first = lax.axis_index("py") * here
    starts = jnp.where(first == 0, 1.0, 0.0)
    ends = jnp.where(first + here == levels, 1.0, 0.0)
    last_row = lax.broadcasted_iota(jnp.int32, (rows, cols), 0) == 0
    blocks = []
    earlier = [before_ref[b] for b in range(pair)]
    for t in range(here):
        for b in range(pair):
            time = aux_ref[0, t, b] - mult_ref[0, t, b]
            if t == here - 1:
                time = time * (1.0 - ends)
            along = aux_ref[1, t, b] - mult_ref[1, t, b]
            second = aux_ref[2, t, b] - mult_ref[2, t, b]
            beside = jnp.where(last_row, rim_ref[t, b], pltpu.roll(along, 1, 0))
            total = (earlier[b] - time) + (beside - along) + (pltpu.roll(second, 1, 1) - second)
            if t == 0:
                total = total - start_ref[b] * starts
            if t == here - 1:
                total = total + end_ref[b] * ends
            earlier[b] = time
            blocks.append(total)
    field = halves(jnp.concatenate(blocks, axis=0))
    modes = dot3((hart_ref[0], hart_ref[1]), field, ((1,), (1,)))
    out_ref[...] = modes.reshape(out_ref.shape)


def solve_kernel(in_ref, hart_ref, table_ref, out_ref, field_ref, factor_ref, sem):
    row_blocks, time_blocks, width, lanes = in_ref.shape
    pieces = lanes // width
    levels, pair, _, cols = field_ref.shape
    here = levels // time_blocks
    half = levels // 2
    mine = lax.axis_index("grp") * lax.axis_size("px") + lax.axis_index("px")
    fetch = pltpu.make_async_copy(table_ref.at[mine], factor_ref, sem)
    fetch.start()
    hart = (hart_ref[0], hart_ref[1])

    def forward(i, carry):
        groups = [
            exchange_pieces([in_ref[g * pieces + j, i] for j in range(pieces)], width)
            for g in range(row_blocks // pieces)
        ]
        field = jnp.concatenate(
            [jnp.concatenate([group[j] for group in groups], axis=1) for j in range(pieces)], axis=0
        )
        modes = dot3(halves(field), hart, ((1,), (0,)))
        field_ref[pl.ds(i * here, here)] = modes.reshape(here, pair, width, cols)
        return carry

    lax.fori_loop(0, time_blocks, forward, 0)
    fetch.wait()

    corner = (8, 128)
    zero = (
        (lax.broadcasted_iota(jnp.int32, corner, 0) == 0)
        & (lax.broadcasted_iota(jnp.int32, corner, 1) == 0)
        & (mine == 0)
    )

    def remove_mean():
        for b in range(pair):
            sums = field_ref[0, b, :8, :128]
            for t in range(1, levels):
                sums = sums + field_ref[t, b, :8, :128]
            mean = jnp.where(zero, sums * (1.0 / levels), 0.0)
            for t in range(levels):
                field_ref[t, b, :8, :128] = field_ref[t, b, :8, :128] - mean

    @pl.when(mine == 0)
    def _():
        remove_mean()

    left = jnp.zeros(field_ref.shape[1:], jnp.float32)
    right = left
    for t in range(half):
        factor = factor_ref[t][None]
        left = (field_ref[t] + left) * factor
        right = (field_ref[levels - 1 - t] + right) * factor
        if t < half - 1:
            field_ref[t] = left
            field_ref[levels - 1 - t] = right
    first = (left + factor * right) * factor_ref[half][None]
    right = right + factor * first
    left = first
    field_ref[half - 1] = left
    field_ref[half] = right
    for t in range(half - 2, -1, -1):
        factor = factor_ref[t][None]
        left = field_ref[t] + factor * left
        right = field_ref[levels - 1 - t] + factor * right
        field_ref[t] = left
        field_ref[levels - 1 - t] = right

    @pl.when(mine == 0)
    def _():
        remove_mean()

    def backward(i, carry):
        field = field_ref[pl.ds(i * here, here)].reshape(here * pair * width, cols)
        modes = dot3(hart, halves(field), ((1,), (1,)))
        out_ref[:, i] = modes.reshape(row_blocks, width, lanes)
        return carry

    lax.fori_loop(0, time_blocks, backward, 0)


def potential_kernel(in_ref, hart_ref, out_ref):
    col_blocks, _, width, lanes = in_ref.shape
    pieces = lanes // width
    groups = [
        exchange_pieces([in_ref[g * pieces + j, 0] for j in range(pieces)], width)
        for g in range(col_blocks // pieces)
    ]
    field = jnp.concatenate(
        [jnp.concatenate([group[j] for group in groups], axis=1) for j in range(pieces)], axis=0
    )
    values = dot3(halves(field), (hart_ref[0], hart_ref[1]), ((1,), (0,)))
    out_ref[...] = values.reshape(out_ref.shape)


def step_kernel(levels, mult_ref, phi_ref, later_ref, below_ref, mult_out, aux_out):
    here, pair, rows, cols = phi_ref.shape
    first = lax.axis_index("py") * here
    inner = jnp.where(first + here == levels, 0.0, 1.0)
    last_row = lax.broadcasted_iota(jnp.int32, (rows, cols), 0) == rows - 1
    for t in range(here):
        for b in range(pair):
            phi = phi_ref[t, b]
            if t < here - 1:
                time_rate = phi_ref[t + 1, b] - phi
            else:
                time_rate = (later_ref[b] - phi) * inner
            below = jnp.where(last_row, below_ref[t, b], pltpu.roll(phi, rows - 1, 0))
            gradient = (time_rate, below - phi, pltpu.roll(phi, cols - 1, 1) - phi)
            mult = [mult_ref[c, t, b] for c in range(3)]
            time_part, one, two = (g + m for g, m in zip(gradient, mult))
            kinetic = 0.5 * (one * one + two * two)
            center = 1.0 + time_part
            scaling = jnp.maximum(center, 1.0) + jnp.exp(jnp.log(kinetic) * (1.0 / 3.0))
            for _ in range(NEWTON):
                residue = scaling * scaling * (scaling - center) - kinetic
                derivative = scaling * (3.0 * scaling - 2.0 * center)
                scaling = jnp.maximum(scaling - residue / derivative, 1.0)
            feasible = time_part + kinetic <= 0.0
            shrink = jnp.where(feasible, 1.0, 1.0 / scaling)
            fresh = (
                jnp.where(feasible, time_part, time_part - (scaling - 1.0)),
                one * shrink,
                two * shrink,
            )
            for c in range(3):
                aux_out[c, t, b] = fresh[c]
                mult_out[c, t, b] = mult[c] + (gradient[c] - fresh[c])


def params():
    return pltpu.CompilerParams(vmem_limit_bytes=VMEM_BYTES)


def local(multiplier, auxiliary, density_start, density_end):
    _, here, batch, rows, cols = multiplier.shape
    time_blocks = lax.axis_size("py")
    row_blocks = lax.axis_size("grp") * lax.axis_size("px")
    levels = here * time_blocks
    row_count = rows * row_blocks
    pair = batch // time_blocks
    width = cols // row_blocks
    lanes = here * pair * rows
    hart_cols = table_halves(cols)
    hart_rows = table_halves(row_count)
    factors = elimination_table(levels, row_count, cols, row_blocks)

    before = moved(auxiliary[0, here - 1] - multiplier[0, here - 1], "py", 1, False)
    rim = moved(
        auxiliary[1, :, :, rows - 1 :] - multiplier[1, :, :, rows - 1 :], ROWS, 1, True
    )
    five = pl.BlockSpec((3, here, pair, rows, cols), lambda p: (0, 0, p, 0, 0))
    plane = pl.BlockSpec((pair, rows, cols), lambda p: (p, 0, 0))
    edge = pl.BlockSpec((here, pair, 1, cols), lambda p: (0, p, 0, 0))
    table = pl.BlockSpec((2, cols, cols), lambda p: (0, 0, 0))
    chunks = pl.BlockSpec((row_blocks, 1, width, lanes), lambda p: (0, p, 0, 0))
    chunked = jax.ShapeDtypeStruct((row_blocks, time_blocks, width, lanes), jnp.float32)
    modes = pl.pallas_call(
        functools.partial(source_kernel, levels),
        grid=(time_blocks,),
        in_specs=[five, five, plane, plane, plane, edge, table],
        out_specs=chunks,
        out_shape=chunked,
        compiler_params=params(),
        name="source",
    )(multiplier, auxiliary, density_start, density_end, before, rim, hart_cols)

    def spread(value):
        flat = value.reshape((row_blocks * time_blocks,) + value.shape[2:])
        return lax.all_to_all(flat, EVERY, 0, 0, tiled=True).reshape(value.shape)

    solved = pl.pallas_call(
        solve_kernel,
        in_specs=[
            pl.BlockSpec(memory_space=pltpu.VMEM),
            pl.BlockSpec(memory_space=pltpu.VMEM),
            pl.BlockSpec(memory_space=pl.ANY),
        ],
        out_specs=pl.BlockSpec(memory_space=pltpu.VMEM),
        out_shape=jax.ShapeDtypeStruct((row_blocks, time_blocks, rows, here * pair * width), jnp.float32),
        scratch_shapes=[
            pltpu.VMEM((levels, pair, width, row_count), jnp.float32),
            pltpu.VMEM(factors.shape[1:], jnp.float32),
            pltpu.SemaphoreType.DMA,
        ],
        compiler_params=params(),
        name="solve",
    )(spread(modes), hart_rows, factors)

    phi_block = pl.BlockSpec((here, pair, rows, cols), lambda p: (0, p, 0, 0))
    back = spread(solved)
    potential = pl.pallas_call(
        potential_kernel,
        grid=(time_blocks,),
        in_specs=[
            pl.BlockSpec((row_blocks, 1, rows, here * pair * width), lambda p: (0, p, 0, 0)),
            table,
        ],
        out_specs=phi_block,
        out_shape=jax.ShapeDtypeStruct((here, batch, rows, cols), jnp.float32),
        compiler_params=params(),
        name="potential",
    )(back, hart_cols)
    later = moved(potential[0], "py", -1, False)
    below = moved(potential[:, :, :1], ROWS, -1, True)
    result = jax.ShapeDtypeStruct(multiplier.shape, jnp.float32)
    mult_next, aux_next = pl.pallas_call(
        functools.partial(step_kernel, levels),
        grid=(time_blocks,),
        in_specs=[five, phi_block, plane, edge],
        out_specs=[five, five],
        out_shape=[result, result],
        compiler_params=params(),
        name="step",
    )(multiplier, potential, later, below)
    return mult_next, aux_next


def solution(mesh):
    field = P(None, "py", None, ROWS, None)
    density = P(None, ROWS, None)
    return jax.shard_map(
        local,
        mesh=mesh,
        in_specs=(field, field, density, density),
        out_specs=(field, field),
        check_vma=False,
    )
```

profile of v0, /device:TPU:1, one launch (start us, length us, event | category | flops | bytes accessed | tf_op | source)
XLA Modules:
  0.0 98.1 jit_solution(13867656207313879551)
XLA Ops:
  0.6 1.1 %subtract_bitcast_fusion = f32[16,16,256]{2,1,0:T(8,128)S(1)} fusion(f32[3,4,16,16,256]{4,3,2,1,0:T(8,128)} %mult_ref.3, f32[3,4,16,16,256]{4,3,2,1,0:T(8,128)} %aux_ref.1), kind=kLoop, calls=%fused_computation.1 | loop fusion | flops 65536 | bytes 786432 | tf_op jit(solution)/shard_map/sub | solution.py:257
  1.7 4.9 %collective-permute-start = (f32[16,16,256]{2,1,0:T(8,128)S(1)}, f32[16,16,256]{2,1,0:T(8,128)S(1)}, u32[]{:S(2)}, u32[]{:S(2)}) collective-permute-start(f32[16,16,256]{2,1,0:T(8,128)S(1)} %subtract_bitcast_fusion), channel_id=1, source_target_pairs={{0,1},{1,2},{2,3},{3,4},{4,5},{5,6},{6,7},{8,9},{9,10},{10,11},{11... | collective-permute-start | bytes 786440 | tf_op jit(solution)/shard_map/ppermute | solution.py:21
  6.6 1.3 %subtract_bitcast_fusion.1 = f32[4,16,1,256]{3,2,1,0:T(1,128)S(1)} fusion(f32[3,4,16,16,256]{4,3,2,1,0:T(8,128)} %mult_ref.3, f32[3,4,16,16,256]{4,3,2,1,0:T(8,128)} %aux_ref.1), kind=kLoop, calls=%fused_computation.2 | loop fusion | flops 16384 | bytes 196608 | tf_op jit(solution)/shard_map/sub | solution.py:259
  7.9 1.4 %collective-permute-start.1 = (f32[4,16,1,256]{3,2,1,0:T(1,128)S(1)}, f32[4,16,1,256]{3,2,1,0:T(1,128)S(1)}, u32[]{:S(2)}, u32[]{:S(2)}) collective-permute-start(f32[4,16,1,256]{3,2,1,0:T(1,128)S(1)} %subtract_bitcast_fusion.1), channel_id=1, source_target_pairs={{0,8},{8,16},{16,24},{24,32},{32,40},{40,48},{48,56},{56,64},{64,7... | collective-permute-start | bytes 196616 | tf_op jit(solution)/shard_map/ppermute | solution.py:21
  9.3 5.3 %collective-permute-done.1.rim_ref = f32[4,16,1,256]{3,2,1,0:T(1,128)S(1)} collective-permute-done((f32[4,16,1,256]{3,2,1,0:T(1,128)S(1)}, f32[4,16,1,256]{3,2,1,0:T(1,128)S(1)}, u32[]{:S(2)}, u32[]{:S(2)}) %collective-permute-start.1) | collective-permute-done | bytes 65568 | tf_op jit(solution)/shard_map/ppermute | solution.py:21
  14.6 0.0 collective-permute-done.before_ref
  14.6 0.0 copy-start
  14.6 1.9 %copy-done = f32[3,4,16,16,256]{4,3,2,1,0:T(8,128)S(1)} copy-done((f32[3,4,16,16,256]{4,3,2,1,0:T(8,128)S(1)}, f32[3,4,16,16,256]{4,3,2,1,0:T(8,128)}, u32[]{:S(2)}) %copy-start) | copy-done | bytes 3145752
  16.5 0.0 copy-start.2
  16.5 0.9 copy-done.2
  17.4 0.0 copy-start.3
  17.4 0.9 copy-done.3
  18.4 0.0 copy-start.4
  18.4 0.9 copy-done.4
  19.3 6.0 %source.1 = f32[16,8,16,128]{3,2,1,0:T(8,128)S(1)} custom-call(f32[3,4,16,16,256]{4,3,2,1,0:T(8,128)S(1)} %copy-done, f32[3,4,16,16,256]{4,3,2,1,0:T(8,128)} %aux_ref.1, f32[16,16,256]{2,1,0:T(8,128)S(1)} %copy-done.3, f32[16,16,256]{2,1,0:T(8,128)S(1)} %copy-done.4, f32[16,16,256]{2,1,0:T(8,128)S(1)} %collective-permute-done.before_ref, ...), custom_call_target="tpu_custom_call" | custom-call | tf_op jit(solution)/shard_map/source/pallas_call | solution.py:267
  25.4 26.4 %all_to_all.10 = f32[128,16,128]{2,1,0:T(8,128)S(1)} all-to-all(f32[128,16,128]{2,1,0:T(8,128)S(1)} %bitcast.13), channel_id=1, replica_groups=mesh['grp'=2,'px'=8,'py'=8] {'grp','px','py'}, dimensions={0} | all-to-all | bytes 2097152 | tf_op jit(solution)/shard_map/all_to_all | solution.py:279
  51.8 5.7 %solve.1 = f32[16,8,16,128]{3,2,1,0:T(8,128)S(1)} custom-call(f32[16,8,16,128]{3,2,1,0:T(8,128)S(1)} %bitcast.11, bf16[2,256,256]{2,1,0:T(8,128)(2,1)S(1)} %copy-done.2, f32[16,17,16,256]{3,2,1,0:T(8,128)} %constant.5.clone.table_ref), custom_call_target="tpu_custom_call" | custom-call | tf_op jit(solution)/shard_map/solve/pallas_call | solution.py:281
  57.5 0.0 copy-start.1
  57.5 23.5 %all_to_all.11 = f32[128,16,128]{2,1,0:T(8,128)S(1)} all-to-all(f32[128,16,128]{2,1,0:T(8,128)S(1)} %bitcast.12), channel_id=1, replica_groups=mesh['grp'=2,'px'=8,'py'=8] {'grp','px','py'}, dimensions={0} | all-to-all | bytes 2097152 | tf_op jit(solution)/shard_map/all_to_all | solution.py:279
  80.9 3.4 %potential.1.phi_ref = f32[4,16,16,256]{3,2,1,0:T(8,128)S(1)} custom-call(f32[16,8,16,128]{3,2,1,0:T(8,128)S(1)} %bitcast.10, bf16[2,256,256]{2,1,0:T(8,128)(2,1)S(1)} %copy-done.2), custom_call_target="tpu_custom_call" | custom-call | tf_op jit(solution)/shard_map/potential/pallas_call | solution.py:301
  84.4 2.3 %collective-permute-start.2 = (f32[16,16,256]{2,1,0:T(8,128)S(1)}, f32[16,16,256]{2,1,0:T(8,128)S(1)}, u32[]{:S(2)}, u32[]{:S(2)}) collective-permute-start(f32[16,16,256]{2,1,0:T(8,128)S(1)} %slice_bitcast_fusion), channel_id=1, source_target_pairs={{1,0},{2,1},{3,2},{4,3},{5,4},{6,5},{7,6},{9,8},{10,9},{11,10},{12... | collective-permute-start | bytes 786440 | tf_op jit(solution)/shard_map/ppermute | solution.py:21
  86.7 2.1 %collective-permute-start.3 = (f32[4,16,1,256]{3,2,1,0:T(1,128)S(1)}, f32[4,16,1,256]{3,2,1,0:T(1,128)S(1)}, u32[]{:S(2)}, u32[]{:S(2)}) collective-permute-start(f32[4,16,1,256]{3,2,1,0:T(1,128)S(1)} %slice.25), channel_id=1, source_target_pairs={{0,120},{8,0},{16,8},{24,16},{32,24},{40,32},{48,40},{56,48},{64,5... | collective-permute-start | bytes 196616 | tf_op jit(solution)/shard_map/ppermute | solution.py:21
  88.9 1.8 %collective-permute-done.3.below_ref = f32[4,16,1,256]{3,2,1,0:T(1,128)S(1)} collective-permute-done((f32[4,16,1,256]{3,2,1,0:T(1,128)S(1)}, f32[4,16,1,256]{3,2,1,0:T(1,128)S(1)}, u32[]{:S(2)}, u32[]{:S(2)}) %collective-permute-start.3) | collective-permute-done | bytes 65568 | tf_op jit(solution)/shard_map/ppermute | solution.py:21
  90.7 1.4 %collective-permute-done.2.later_ref = f32[16,16,256]{2,1,0:T(8,128)S(1)} collective-permute-done((f32[16,16,256]{2,1,0:T(8,128)S(1)}, f32[16,16,256]{2,1,0:T(8,128)S(1)}, u32[]{:S(2)}, u32[]{:S(2)}) %collective-permute-start.2) | collective-permute-done | bytes 262176 | tf_op jit(solution)/shard_map/ppermute | solution.py:21
  92.1 0.0 copy-done.1
  92.1 6.0 %step.1 = (f32[3,4,16,16,256]{4,3,2,1,0:T(8,128)}, f32[3,4,16,16,256]{4,3,2,1,0:T(8,128)}) custom-call(f32[3,4,16,16,256]{4,3,2,1,0:T(8,128)S(1)} %copy-done.1, f32[4,16,16,256]{3,2,1,0:T(8,128)S(1)} %potential.1.phi_ref, f32[16,16,256]{2,1,0:T(8,128)S(1)} %collective-permute-done.2.later_ref, f32[4,16,1,256]{3,2,1,0:T(1,128)S(1)} %collective-permute-done.3.below_ref), custom_call_target="tpu_custom_call" | custom-call | tf_op jit(solution)/shard_map/step/pallas_call | solution.py:316
  (2 shorter events, 0.1 us)
Async XLA Ops:
  1.7 12.9 %collective-permute-start = (f32[16,16,256]{2,1,0:T(8,128)S(1)}, f32[16,16,256]{2,1,0:T(8,128)S(1)}, u32[]{:S(2)}, u32[]{:S(2)}) collective-permute-start(f32[16,16,256]{2,1,0:T(8,128)S(1)} %subtract_bitcast_fusion), channel_id=1, source_target_pairs={{0,1},{1,2},{2,3},{3,4},{4,5},{5,6},{6,7},{8,9},{9,10},{10,11},{11... | collective-permute-start | bytes 786440 | tf_op jit(solution)/shard_map/ppermute | solution.py:21
  7.9 6.7 %collective-permute-start.1 = (f32[4,16,1,256]{3,2,1,0:T(1,128)S(1)}, f32[4,16,1,256]{3,2,1,0:T(1,128)S(1)}, u32[]{:S(2)}, u32[]{:S(2)}) collective-permute-start(f32[4,16,1,256]{3,2,1,0:T(1,128)S(1)} %subtract_bitcast_fusion.1), channel_id=1, source_target_pairs={{0,8},{8,16},{16,24},{24,32},{32,40},{40,48},{48,56},{56,64},{64,7... | collective-permute-start | bytes 196616 | tf_op jit(solution)/shard_map/ppermute | solution.py:21
  14.6 1.9 %copy-start = (f32[3,4,16,16,256]{4,3,2,1,0:T(8,128)S(1)}, f32[3,4,16,16,256]{4,3,2,1,0:T(8,128)}, u32[]{:S(2)}) copy-start(f32[3,4,16,16,256]{4,3,2,1,0:T(8,128)} %mult_ref.3) | copy-start | bytes 9437188
  16.5 0.9 copy-start.2
  17.4 0.9 copy-start.3
  18.4 0.9 copy-start.4
  57.5 34.6 %copy-start.1 = (f32[3,4,16,16,256]{4,3,2,1,0:T(8,128)S(1)}, f32[3,4,16,16,256]{4,3,2,1,0:T(8,128)}, u32[]{:S(2)}) copy-start(f32[3,4,16,16,256]{4,3,2,1,0:T(8,128)} %mult_ref.3) | copy-start | bytes 9437188
  84.4 7.7 %collective-permute-start.2 = (f32[16,16,256]{2,1,0:T(8,128)S(1)}, f32[16,16,256]{2,1,0:T(8,128)S(1)}, u32[]{:S(2)}, u32[]{:S(2)}) collective-permute-start(f32[16,16,256]{2,1,0:T(8,128)S(1)} %slice_bitcast_fusion), channel_id=1, source_target_pairs={{1,0},{2,1},{3,2},{4,3},{5,4},{6,5},{7,6},{9,8},{10,9},{11,10},{12... | collective-permute-start | bytes 786440 | tf_op jit(solution)/shard_map/ppermute | solution.py:21
  86.7 4.0 %collective-permute-start.3 = (f32[4,16,1,256]{3,2,1,0:T(1,128)S(1)}, f32[4,16,1,256]{3,2,1,0:T(1,128)S(1)}, u32[]{:S(2)}, u32[]{:S(2)}) collective-permute-start(f32[4,16,1,256]{3,2,1,0:T(1,128)S(1)} %slice.25), channel_id=1, source_target_pairs={{0,120},{8,0},{16,8},{24,16},{32,24},{40,32},{48,40},{56,48},{64,5... | collective-permute-start | bytes 196616 | tf_op jit(solution)/shard_map/ppermute | solution.py:21
where the time goes:
time: 98.5 us; the launch traced here: 98.1 us
  blocking collectives  49.8 us (51%)
  Pallas kernels  21.2 us (22%)
  starting transfers between devices  10.7 us (11%)
  waiting for transfers between devices  8.49 us (9%)
  local copies, waits for them, and re-layouts  4.8 us (5%)
  other arithmetic  2.37 us (2%)
    all_to_all x2, blocking collectives, spread(): return lax.all_to_all(flat, EVERY, 0, 0, tiled=True).reshape(value.shape)  49.8 us
    ppermute x4, starting transfers between devices, moved(): return lax.ppermute(value, axis, pairs)  10.7 us
    ppermute x4, waiting for transfers between devices, moved(): return lax.ppermute(value, axis, pairs)  8.49 us
    pallas_call x1, Pallas kernels, local(): pl.pallas_call(functools.partial(source_kernel, levels), grid=(time_block...  6.03 us
    pallas_call x1, Pallas kernels, local(): pl.pallas_call(functools.partial(step_kernel, levels), grid=(time_blocks,...  6.01 us
    pallas_call x1, Pallas kernels, local(): pl.pallas_call(solve_kernel, in_specs=[pl.BlockSpec(memory_space=pltpu.VM...  5.69 us
    unnamed x10, local copies, waits for them, and re-layouts  4.75 us
    pallas_call x1, Pallas kernels, local(): pl.pallas_call(potential_kernel, grid=(time_blocks,), in_specs=[pl.BlockS...  3.42 us
  transfers between devices with their start and end apart: 4, of which 3 were waited for; matrix products, arithmetic and copies ran while one was open for 1% of the time, Pallas kernels for 0%

commit v1 on v0

v1 whole, which is shorter than its diff:
```python
import functools

import jax
import jax.numpy as jnp
import numpy as np
from jax import lax
from jax.experimental import pallas as pl
from jax.experimental.pallas import tpu as pltpu
from jax.sharding import PartitionSpec as P

NEWTON = 4
ROWS = ("grp", "px")
EVERY = ("grp", "px", "py")
GROUP = 2
VMEM_BYTES = 48 * 1024 * 1024
DIRECT = ((1,), (0,))
CROSS = ((1,), (1,))


def table_parts(table, count):
    rest = np.asarray(table, np.float32)
    parts = []
    for _ in range(count):
        parts.append(rest.astype(jnp.bfloat16))
        rest = rest - parts[-1].astype(np.float32)
    return np.stack(parts)


def parts_of(value, count):
    parts = [value.astype(jnp.bfloat16)]
    for _ in range(count - 1):
        value = value - parts[-1].astype(jnp.float32)
        parts.append(value.astype(jnp.bfloat16))
    return parts


def product(left, right, dims):
    total = None
    count = len(left)
    for order in range(count - 1, -1, -1):
        for i in range(order + 1):
            term = lax.dot_general(
                left[i], right[order - i], (dims, ((), ())), preferred_element_type=jnp.float32
            )
            total = term if total is None else total + term
    return total


def table_list(ref, *index):
    return [ref[index + (i,)] for i in range(ref.shape[len(index)])]


def squared_sines(length, period):
    return 4.0 * np.sin(np.pi * np.arange(length) / period) ** 2


def hartley_table(length):
    index = np.arange(length)
    angles = (index[:, None] * index[None, :] % length) * (2.0 * np.pi / length)
    return (np.cos(angles) + np.sin(angles)) / np.sqrt(length)


def elimination_table(levels, row_count, col_count, blocks):
    eigen = squared_sines(col_count, col_count)[:, None] + squared_sines(row_count, row_count)
    factors = [1.0 / (1.0 + eigen)]
    for _ in range(levels // 2 - 1):
        factors.append(1.0 / (2.0 + eigen - factors[-1]))
    gap = 1.0 - factors[-1] ** 2
    middle = np.where(eigen > 0.0, 1.0 / np.where(eigen > 0.0, gap, 1.0), 0.0)
    table = np.stack(factors + [middle]).astype(np.float32)
    table = table.reshape(levels // 2 + 1, blocks, col_count // blocks, row_count)
    return np.ascontiguousarray(table.transpose(1, 0, 2, 3))


def slots(here, rows, b, kind, index):
    if kind == "level":
        return b * rows + index
    if kind == "later":
        return (2 + b) * rows + index
    base = 4 * rows + b * (rows // 2)
    return base + (index - 1 if kind == "row" else here - 1 + index)


def interior_tables(here, rows, cols, last):
    pair = 2
    lanes = here * pair * rows
    inner = here - 1
    chain = 2.0 * np.eye(inner) - np.eye(inner, k=1) - np.eye(inner, k=-1)
    if last:
        chain[-1, -1] = 1.0
    time_values, time_basis = np.linalg.eigh(chain)
    row_index = np.arange(1, rows)
    row_basis = np.sqrt(2.0 / rows) * np.sin(np.pi * np.outer(row_index, row_index) / rows)
    row_values = squared_sines(rows, 2 * rows)
    col_values = squared_sines(cols, cols)
    basis = np.zeros((here, pair, rows, here, pair, rows))
    inverse = np.zeros((cols, here, pair, rows))
    linked = np.zeros((here, pair, rows, lanes))
    for b in range(pair):
        for k in range(1, here):
            for t in range(1, here):
                basis[t, b, 1:, k, b, 1:] = time_basis[t - 1, k - 1] * row_basis
            inverse[:, k, b, 1:] = 1.0 / (
                col_values[:, None] + time_values[k - 1] + row_values[None, 1:]
            )
        for x in range(1, rows):
            linked[1, b, x, slots(here, rows, b, "level", x)] = 1.0
            if not last:
                linked[here - 1, b, x, slots(here, rows, b, "later", x)] = 1.0
        for t in range(1, here):
            linked[t, b, 1, slots(here, rows, b, "row", t)] = 1.0
            linked[t, b, rows - 1, slots(here, rows, b, "next", t)] = 1.0
    basis = basis.reshape(lanes, lanes)
    linked = linked.reshape(lanes, lanes)
    inverse = inverse.reshape(cols, lanes)
    to_edges = basis.T @ linked
    from_edges = to_edges.T.copy()
    for b in range(pair):
        ones = np.zeros((here, pair, rows))
        ones[1:, b, 1:] = 1.0
        from_edges[slots(here, rows, b, "next", here)] = -(ones.reshape(-1) @ basis)
    return basis, inverse, to_edges, from_edges


def constant_source(here, rows, time_blocks, row_blocks, tables):
    levels, row_count = here * time_blocks, rows * row_blocks
    field = np.zeros((levels + 1, row_count))
    ones = np.zeros((here, 2, rows))
    ones[1:, 0, 1:] = 1.0
    for i in range(time_blocks):
        basis, inverse, to_edges, _ = tables[1 if i == time_blocks - 1 else 0]
        edge = ((ones.reshape(-1) @ basis) * inverse[0]) @ to_edges
        for j in range(row_blocks):
            t0, x0 = i * here, j * rows
            for x in range(rows):
                field[t0, x0 + x] += 1.0 + edge[slots(here, rows, 0, "level", x)]
                field[t0 + here, x0 + x] += edge[slots(here, rows, 0, "later", x)]
            for t in range(here):
                after = (x0 + rows) % row_count
                field[t0 + t, after] += edge[slots(here, rows, 0, "next", t)]
                if t > 0:
                    field[t0 + t, x0] += 1.0 + edge[slots(here, rows, 0, "row", t)]
    return field[:levels] @ hartley_table(row_count)


def exchange_pieces(blocks, width):
    count = len(blocks)
    lanes = count * width
    group = lax.broadcasted_iota(jnp.int32, blocks[0].shape, 1) // width
    step = 1
    while step < count:
        upper = (group // step) % 2 == 1
        fresh = list(blocks)
        for j in range(count):
            if (j // step) % 2 == 0:
                low, high = blocks[j], blocks[j + step]
                fresh[j] = jnp.where(upper, pltpu.roll(high, step * width, 1), low)
                fresh[j + step] = jnp.where(upper, high, pltpu.roll(low, lanes - step * width, 1))
        blocks = fresh
        step *= 2
    return blocks


def source_kernel(
    levels,
    pair,
    mult_ref,
    aux_ref,
    start_hbm,
    end_hbm,
    hart_hbm,
    basis_hbm,
    inverse_hbm,
    edges_hbm,
    out_ref,
    inner_ref,
    density_ref,
    hart_ref,
    basis_ref,
    inverse_ref,
    edges_ref,
    sems,
):
    _, here, batch, rows, cols = mult_ref.shape
    first = lax.axis_index("py") * here
    last = (first + here == levels).astype(jnp.int32)
    step = pl.program_id(0)

    @pl.when(step == 0)
    def _():
        copies = [
            pltpu.make_async_copy(hart_hbm, hart_ref, sems.at[0]),
            pltpu.make_async_copy(basis_hbm.at[last], basis_ref, sems.at[1]),
            pltpu.make_async_copy(inverse_hbm.at[last], inverse_ref, sems.at[2]),
            pltpu.make_async_copy(edges_hbm.at[last], edges_ref, sems.at[3]),
            pltpu.make_async_copy(start_hbm, density_ref.at[0], sems.at[4]),
            pltpu.make_async_copy(end_hbm, density_ref.at[1], sems.at[5]),
        ]
        for copy in copies:
            copy.start()
        for copy in copies:
            copy.wait()

    for q in range(batch // pair):
        source_part(
            first, last, q, step * batch + q * pair, pair, mult_ref, aux_ref, density_ref,
            hart_ref, basis_ref, inverse_ref, edges_ref, out_ref, inner_ref,
        )


def source_part(
    first, last, q, problem, pair, mult_ref, aux_ref, density_ref,
    hart_ref, basis_ref, inverse_ref, edges_ref, out_ref, inner_ref,
):
    here, _, rows, cols = mult_ref.shape[1:]
    lanes = here * pair * rows
    starts = jnp.where(first == 0, 1.0, 0.0)
    ends = last.astype(jnp.float32)
    row_index = lax.broadcasted_iota(jnp.int32, (rows, cols), 0)
    first_row = row_index == 0
    blocks = []
    earlier = [0.0] * pair
    rims = jnp.zeros((rows, cols), jnp.float32)
    for t in range(here):
        for b in range(pair):
            time = aux_ref[0, t, q * pair + b] - mult_ref[0, t, q * pair + b]
            if t == here - 1:
                time = time * (1.0 - ends)
            along = aux_ref[1, t, q * pair + b] - mult_ref[1, t, q * pair + b]
            second = aux_ref[2, t, q * pair + b] - mult_ref[2, t, q * pair + b]
            beside = jnp.where(first_row, 0.0, pltpu.roll(along, 1, 0))
            total = (earlier[b] - time) + (beside - along) + (pltpu.roll(second, 1, 1) - second)
            if t == 0:
                total = total - density_ref[0, problem + b] * starts
            if t == here - 1:
                total = total + density_ref[1, problem + b] * ends
            earlier[b] = time
            blocks.append(total)
            base = b * (rows // 2)
            if t > 0:
                rims = jnp.where(row_index == base + t - 1, total[:1], rims)
            rims = jnp.where(row_index == base + here - 1 + t, along[rows - 1 :], rims)
    spare = jnp.zeros((lanes - (2 * pair + 1) * rows, cols), jnp.float32)
    nodes = jnp.concatenate(blocks + blocks[:pair] + earlier + [rims, spare], axis=0)
    modes = product(table_list(hart_ref), parts_of(nodes, 2), CROSS)
    inner = product(parts_of(modes[:, :lanes], 2), table_list(basis_ref), DIRECT)
    inner_ref[q] = inner
    gone = parts_of(inner * inverse_ref[...], 2)
    edges = modes[:, lanes:] + product(gone, table_list(edges_ref), DIRECT)
    out_ref[:, q] = edges.reshape(out_ref.shape[0], out_ref.shape[2], lanes)


def solve_kernel(in_ref, hart_ref, ones_ref, table_ref, out_ref, field_ref, mean_ref, factor_ref, sem):
    row_blocks, time_blocks, width, lanes = in_ref.shape
    pieces = lanes // width
    levels, pair, _, cols = field_ref.shape
    here = levels // time_blocks
    rows = cols // row_blocks
    half = levels // 2
    mine = lax.axis_index("grp") * lax.axis_size("px") + lax.axis_index("px")
    fetch = pltpu.make_async_copy(table_ref.at[mine], factor_ref, sem)
    fetch.start()
    hart = table_list(hart_ref)
    corner = lax.broadcasted_iota(jnp.int32, (width, cols), 1) % rows == 0

    def shift(value, steps):
        return pltpu.roll(value, steps % cols, 1)

    def offset(b, kind, t):
        return slots(here, rows, b, kind, t) - 4 * rows

    def forward(i, carry):
        groups = [
            exchange_pieces([in_ref[g * pieces + j, i] for j in range(pieces)], width)
            for g in range(row_blocks // pieces)
        ]
        kinds = [jnp.concatenate([group[k] for group in groups], axis=1) for k in range(5)]
        rims = kinds[4]
        field = []
        for t in range(here):
            for b in range(pair):
                value = shift(rims, rows - offset(b, "next", t))
                if t > 0:
                    value = value + shift(rims, -offset(b, "row", t))
                value = jnp.where(corner, value, 0.0)
                if t == 0:
                    value = value + kinds[b] + carry[b]
                field.append(value)
        field = jnp.concatenate(field, axis=0)
        modes = product(parts_of(field, 2), hart[:2], DIRECT)
        field_ref[pl.ds(i * here, here)] = modes.reshape(here, pair, width, cols)
        return tuple(kinds[2 : 2 + pair])

    blank = jnp.zeros((width, cols), jnp.float32)
    lax.fori_loop(0, time_blocks, forward, (blank,) * pair, unroll=True)
    fetch.wait()

    mean_ref[...] = jnp.zeros(mean_ref.shape, jnp.float32)

    @pl.when(mine == 0)
    def _():
        tile = (8, 128)
        zero = (lax.broadcasted_iota(jnp.int32, tile, 0) == 0) & (
            lax.broadcasted_iota(jnp.int32, tile, 1) == 0
        )
        scale = float(np.sqrt(cols)) / (levels * cols)
        for b in range(pair):
            sums = field_ref[0, b, :8, :128]
            for t in range(1, levels):
                sums = sums + field_ref[t, b, :8, :128]
            mean = jnp.sum(jnp.where(zero, sums * scale, 0.0), axis=1, keepdims=True)
            mean_ref[b, :8] = jnp.broadcast_to(mean, (8, cols))
            for t in range(levels):
                field_ref[t, b, :8] = field_ref[t, b, :8] - mean * ones_ref[t : t + 1]

    left = jnp.zeros(field_ref.shape[1:], jnp.float32)
    right = left
    for t in range(half):
        factor = factor_ref[t][None]
        left = (field_ref[t] + left) * factor
        right = (field_ref[levels - 1 - t] + right) * factor
        if t < half - 1:
            field_ref[t] = left
            field_ref[levels - 1 - t] = right
    first = (left + factor * right) * factor_ref[half][None]
    right = right + factor * first
    left = first
    field_ref[half - 1] = left
    field_ref[half] = right
    for t in range(half - 2, -1, -1):
        factor = factor_ref[t][None]
        left = field_ref[t] + factor * left
        right = field_ref[levels - 1 - t] + factor * right
        field_ref[t] = left
        field_ref[levels - 1 - t] = right

    def backward(step, carry):
        i = time_blocks - 1 - step
        field = field_ref[pl.ds(i * here, here)].reshape(here * pair * width, cols)
        values = product(parts_of(field, 3), hart, DIRECT)
        part = [
            [values[(t * pair + b) * width : (t * pair + b + 1) * width] for b in range(pair)]
            for t in range(here)
        ]
        lane = lax.broadcasted_iota(jnp.int32, (width, cols), 1) % rows
        rims = jnp.zeros((width, cols), jnp.float32)
        for b in range(pair):
            for t in range(here):
                at = offset(b, "next", t)
                rims = jnp.where(lane == at, shift(part[t][b], at - rows), rims)
                if t > 0:
                    at = offset(b, "row", t)
                    rims = jnp.where(lane == at, shift(part[t][b], at), rims)
            rims = jnp.where(lane == offset(b, "next", here), mean_ref[b], rims)
        kinds = part[0] + list(carry) + [rims]
        for g in range(row_blocks // pieces):
            cut = [kind[:, g * lanes : (g + 1) * lanes] for kind in kinds]
            cut += [jnp.zeros((width, lanes), jnp.float32)] * (pieces - len(cut))
            for j, value in enumerate(exchange_pieces(cut, width)):
                out_ref[g * pieces + j, i] = value
        return tuple(part[0])

    lax.fori_loop(0, time_blocks, backward, (blank,) * pair, unroll=True)


def step_kernel(
    levels,
    pair,
    mult_ref,
    edge_ref,
    inner_ref,
    hart_ref,
    links_ref,
    inverse_ref,
    basis_ref,
    mult_out,
    aux_out,
):
    for q in range(mult_ref.shape[2] // pair):
        step_part(
            levels, q, pair, mult_ref, edge_ref, inner_ref, hart_ref, links_ref, inverse_ref,
            basis_ref, mult_out, aux_out,
        )


def step_part(
    levels, q, pair, mult_ref, edge_ref, inner_ref, hart_ref, links_ref, inverse_ref, basis_ref,
    mult_out, aux_out,
):
    here, _, rows, cols = mult_ref.shape[1:]
    lanes = here * pair * rows
    first = lax.axis_index("py") * here
    last = (first + here == levels).astype(jnp.int32)
    inside = 1.0 - last.astype(jnp.float32)
    row_index = lax.broadcasted_iota(jnp.int32, (rows, cols), 0)
    edges = edge_ref[:, q].reshape(cols, lanes)
    linked = product(parts_of(edges, 3), table_list(links_ref, last), DIRECT)
    gone = (inner_ref[q] + linked) * inverse_ref[last]
    nodes = product(parts_of(gone, 3), table_list(basis_ref, last), DIRECT)
    whole = jnp.concatenate([nodes, edges], axis=1).T
    values = product(parts_of(whole, 3), table_list(hart_ref), DIRECT)

    def piece(start, count):
        return values[start : start + count]

    rims = lanes + 4 * rows
    phi = []
    for t in range(here):
        for b in range(pair):
            if t == 0:
                phi.append(piece(lanes + b * rows, rows))
            else:
                row = piece(lanes + slots(here, rows, b, "row", t), 1)
                phi.append(jnp.where(row_index == 0, row, piece((t * pair + b) * rows, rows)))
    for b in range(pair):
        phi.append(piece(lanes + (pair + b) * rows, rows))
    for t in range(here):
        for b in range(pair):
            mine = phi[t * pair + b]
            time_rate = phi[(t + 1) * pair + b] - mine
            if t == here - 1:
                time_rate = time_rate * inside
            row = piece(lanes + slots(here, rows, b, "next", t), 1)
            below = jnp.where(row_index == rows - 1, row, pltpu.roll(mine, rows - 1, 0))
            gradient = (time_rate, below - mine, pltpu.roll(mine, cols - 1, 1) - mine)
            mult = [mult_ref[c, t, q * pair + b] for c in range(3)]
            time_part, one, two = (g + m for g, m in zip(gradient, mult))
            kinetic = 0.5 * (one * one + two * two)
            center = 1.0 + time_part
            scaling = jnp.maximum(center, 1.0) + jnp.exp(jnp.log(kinetic) * (1.0 / 3.0))
            twice = center + center
            for _ in range(NEWTON):
                residue = scaling * scaling * (scaling - center) - kinetic
                derivative = scaling * (3.0 * scaling - twice)
                change = residue * pl.reciprocal(derivative, approx=True)
                scaling = jnp.maximum(scaling - change, 1.0)
            feasible = time_part + kinetic <= 0.0
            shrink = jnp.where(feasible, 1.0, 1.0 / scaling)
            fresh = (
                jnp.where(feasible, time_part, time_part - (scaling - 1.0)),
                one * shrink,
                two * shrink,
            )
            for c in range(3):
                aux_out[c, t, q * pair + b] = fresh[c]
                mult_out[c, t, q * pair + b] = mult[c] + (gradient[c] - fresh[c])


def params(size=48):
    return pltpu.CompilerParams(vmem_limit_bytes=size * 1024 * 1024)


def whole_block(array):
    return pl.BlockSpec(array.shape, lambda p: (0,) * array.ndim)


def local(multiplier, auxiliary, density_start, density_end):
    _, here, batch, rows, cols = multiplier.shape
    time_blocks = lax.axis_size("py")
    row_blocks = lax.axis_size("grp") * lax.axis_size("px")
    levels = here * time_blocks
    row_count = rows * row_blocks
    pair = batch // time_blocks
    width = cols // row_blocks
    lanes = here * pair * rows
    both = [interior_tables(here, rows, cols, last) for last in (False, True)]
    hart_cols = table_parts(hartley_table(cols), 3)
    hart_rows = table_parts(hartley_table(row_count), 3)
    basis2 = np.stack([table_parts(one[0], 2) for one in both])
    basis3 = np.stack([table_parts(one[0].T, 3) for one in both])
    inverse = np.stack([one[1] for one in both]).astype(np.float32)
    to_edges = np.stack([table_parts(one[2], 2) for one in both])
    from_edges = np.stack([table_parts(one[3], 3) for one in both])
    ones = constant_source(here, rows, time_blocks, row_blocks, both).astype(np.float32)
    factors = elimination_table(levels, row_count, cols, row_blocks)

    group = GROUP
    five = pl.BlockSpec((3, here, pair * group, rows, cols), lambda p: (0, 0, p, 0, 0))
    chunks = pl.BlockSpec((row_blocks, group, width, lanes), lambda p: (0, p, 0, 0))
    away = pl.BlockSpec(memory_space=pltpu.HBM)
    chunked = jax.ShapeDtypeStruct((row_blocks, time_blocks, width, lanes), jnp.float32)
    kept = pl.BlockSpec((group, cols, lanes), lambda p: (p, 0, 0))
    edges, inner = pl.pallas_call(
        functools.partial(source_kernel, levels, pair),
        grid=(time_blocks // group,),
        in_specs=[five, five] + [away] * 6,
        out_specs=[chunks, kept],
        out_shape=[chunked, jax.ShapeDtypeStruct((time_blocks, cols, lanes), jnp.float32)],
        scratch_shapes=[
            pltpu.VMEM((2,) + density_start.shape, jnp.float32),
            pltpu.VMEM((2, cols, cols), jnp.bfloat16),
            pltpu.VMEM(basis2.shape[1:], jnp.bfloat16),
            pltpu.VMEM(inverse.shape[1:], jnp.float32),
            pltpu.VMEM(to_edges.shape[1:], jnp.bfloat16),
            pltpu.SemaphoreType.DMA((6,)),
        ],
        compiler_params=params(56),
        name="source",
    )(multiplier, auxiliary, density_start, density_end, hart_cols[:2], basis2, inverse, to_edges)

    def spread(value):
        flat = value.reshape((row_blocks * time_blocks,) + value.shape[2:])
        return lax.all_to_all(flat, EVERY, 0, 0, tiled=True).reshape(value.shape)

    vmem = pl.BlockSpec(memory_space=pltpu.VMEM)
    solved = pl.pallas_call(
        solve_kernel,
        in_specs=[vmem, vmem, vmem, pl.BlockSpec(memory_space=pl.ANY)],
        out_specs=vmem,
        out_shape=chunked,
        scratch_shapes=[
            pltpu.VMEM((levels, pair, width, row_count), jnp.float32),
            pltpu.VMEM((pair, width, row_count), jnp.float32),
            pltpu.VMEM(factors.shape[1:], jnp.float32),
            pltpu.SemaphoreType.DMA,
        ],
        compiler_params=params(),
        name="solve",
    )(spread(edges), hart_rows, ones, factors)

    result = jax.ShapeDtypeStruct(multiplier.shape, jnp.float32)
    mult_next, aux_next = pl.pallas_call(
        functools.partial(step_kernel, levels, pair),
        grid=(time_blocks // group,),
        in_specs=[five, chunks, kept]
        + [whole_block(a) for a in (hart_cols, from_edges, inverse, basis3)],
        out_specs=[five, five],
        out_shape=[result, result],
        compiler_params=params(),
        name="step",
    )(multiplier, spread(solved), inner, hart_cols, from_edges, inverse, basis3)
    return mult_next, aux_next


def solution(mesh):
    field = P(None, "py", None, ROWS, None)
    density = P(None, ROWS, None)
    return jax.shard_map(
        local,
        mesh=mesh,
        in_specs=(field, field, density, density),
        out_specs=(field, field),
        check_vma=False,
    )
```

time: 98.5 us -> 84 us (0.85)
  starting transfers between devices: 10.7 us -> 0 us
  waiting for transfers between devices: 8.49 us -> 0 us
  Pallas kernels: 21.2 us -> 28.5 us
  local copies, waits for them, and re-layouts: 4.8 us -> 0.03 us
  blocking collectives: 49.8 us -> 54.3 us
  other arithmetic: 2.37 us -> 0 us
    ppermute x4 -> x0, starting transfers between devices: 10.7 us -> none  [moved(): return lax.ppermute(value, axis, pairs)]
    ppermute x4 -> x0, waiting for transfers between devices: 8.49 us -> none  [moved(): return lax.ppermute(value, axis, pairs)]
    pallas_call x4 -> x3, Pallas kernels: 21.2 us -> 28.5 us  [the longest x1 13.7 us: local(): pl.pallas_call(functools.partial(step_kernel, levels, pair), grid=(time_b...]
    unnamed x10 -> x12, local copies, waits for them, and re-layouts: 4.75 us -> 0.03 us
    all_to_all x2, blocking collectives: 49.8 us -> 54.3 us  [spread(): return lax.all_to_all(flat, EVERY, 0, 0, tiled=True).reshape(value.shape)]
    sub x2 -> x0, other arithmetic: 2.37 us -> none  [the longest x1 1.3 us: local(): auxiliary[1, :, :, rows - 1:] - multiplier[1, :, :, rows - 1:]]
  transfers between devices with their start and end apart: 4 -> 0, of which waited for: 3 -> 0; matrix products, arithmetic and copies ran while one was open for 1% -> 0% of each run, Pallas kernels for 0% -> 0%
where the time goes in v1:
time: 84 us; the launch traced here: 83.6 us
  blocking collectives  54.3 us (65%)
  Pallas kernels  28.5 us (34%)
    all_to_all x2, blocking collectives, spread(): return lax.all_to_all(flat, EVERY, 0, 0, tiled=True).reshape(value.shape)  54.3 us
    pallas_call x1, Pallas kernels, local(): pl.pallas_call(functools.partial(step_kernel, levels, pair), grid=(time_b...  13.7 us
    pallas_call x1, Pallas kernels, local(): pl.pallas_call(functools.partial(source_kernel, levels, pair), grid=(time...  9.5 us
    pallas_call x1, Pallas kernels, local(): pl.pallas_call(solve_kernel, in_specs=[vmem, vmem, vmem, pl.BlockSpec(mem...  5.35 us

profile of v1, /device:TPU:1, one launch (start us, length us, event | category | flops | bytes accessed | tf_op | source)
XLA Modules:
  0.0 83.6 jit_solution(7670917070802006777)
XLA Ops:
  0.6 0.0 copy-start
  0.6 0.0 copy-start.5
  0.7 9.5 %source.1 = (f32[16,8,16,128]{3,2,1,0:T(8,128)}, f32[8,256,128]{2,1,0:T(8,128)}) custom-call(f32[3,4,16,16,256]{4,3,2,1,0:T(8,128)} %mult_ref.3, f32[3,4,16,16,256]{4,3,2,1,0:T(8,128)} %aux_ref.1, f32[16,16,256]{2,1,0:T(8,128)} %start_hbm.1, f32[16,16,256]{2,1,0:T(8,128)} %end_hbm.1, bf16[2,256,256]{2,1,0:T(8,128)(2,1)} %constant.18.clone.hart_hbm, ...), custom_call_target="tpu_custom_call" | custom-call | tf_op jit(solution)/shard_map/source/pallas_call | solution.py:483
  10.2 30.9 %all_to_all.10 = f32[128,16,128]{2,1,0:T(8,128)S(1)} all-to-all(f32[128,16,128]{2,1,0:T(8,128)} %bitcast.7), channel_id=1, replica_groups=mesh['grp'=2,'px'=8,'py'=8] {'grp','px','py'}, dimensions={0} | all-to-all | bytes 2097152 | tf_op jit(solution)/shard_map/all_to_all | solution.py:503
  41.1 0.0 copy-done
  41.1 0.0 copy-done.5
  41.1 0.0 copy-start.1
  41.1 0.0 copy-start.2
  41.1 0.0 copy-start.3
  41.1 0.0 copy-start.4
  41.1 5.4 %solve.1 = f32[16,8,16,128]{3,2,1,0:T(8,128)S(1)} custom-call(f32[16,8,16,128]{3,2,1,0:T(8,128)S(1)} %bitcast.5, bf16[3,256,256]{2,1,0:T(8,128)(2,1)S(1)} %copy-done, f32[32,256]{1,0:T(8,128)S(1)} %copy-done.5, f32[16,17,16,256]{3,2,1,0:T(8,128)} %constant.24.clone.table_ref), custom_call_target="tpu_custom_call" | custom-call | tf_op jit(solution)/shard_map/solve/pallas_call | solution.py:506
  46.5 23.4 %all_to_all.11 = f32[128,16,128]{2,1,0:T(8,128)S(1)} all-to-all(f32[128,16,128]{2,1,0:T(8,128)S(1)} %bitcast.6), channel_id=1, replica_groups=mesh['grp'=2,'px'=8,'py'=8] {'grp','px','py'}, dimensions={0} | all-to-all | bytes 2097152 | tf_op jit(solution)/shard_map/all_to_all | solution.py:503
  69.9 0.0 copy-done.1
  69.9 0.0 copy-done.2
  69.9 0.0 copy-done.3
  69.9 0.0 copy-done.4
  69.9 13.7 %step.1 = (f32[3,4,16,16,256]{4,3,2,1,0:T(8,128)}, f32[3,4,16,16,256]{4,3,2,1,0:T(8,128)}) custom-call(f32[3,4,16,16,256]{4,3,2,1,0:T(8,128)} %mult_ref.3, f32[16,8,16,128]{3,2,1,0:T(8,128)S(1)} %bitcast.4, f32[8,256,128]{2,1,0:T(8,128)S(1)} %copy-done.1, bf16[3,256,256]{2,1,0:T(8,128)(2,1)S(1)} %copy-done, bf16[2,3,128,128]{3,2,1,0:T(8,128)(2,1)S(1)} %copy-done.4, ...), custom_call_target="tpu_custom_call" | custom-call | tf_op jit(solution)/shard_map/step/pallas_call | solution.py:522
Async XLA Ops:
  0.6 40.4 %copy-start = (bf16[3,256,256]{2,1,0:T(8,128)(2,1)S(1)}, bf16[3,256,256]{2,1,0:T(8,128)(2,1)}, u32[]{:S(2)}) copy-start(bf16[3,256,256]{2,1,0:T(8,128)(2,1)} %constant.22.clone.hart_ref) | copy-start | bytes 1179652
  0.6 40.4 %copy-start.5 = (f32[32,256]{1,0:T(8,128)S(1)}, f32[32,256]{1,0:T(8,128)}, u32[]{:S(2)}) copy-start(f32[32,256]{1,0:T(8,128)} %constant.23.clone.ones_ref) | copy-start | bytes 98308
  41.1 28.8 %copy-start.1 = (f32[8,256,128]{2,1,0:T(8,128)S(1)}, f32[8,256,128]{2,1,0:T(8,128)}, u32[]{:S(2)}) copy-start(f32[8,256,128]{2,1,0:T(8,128)} %get-tuple-element.5.inner_ref) | copy-start | bytes 3145732
  41.1 28.8 %copy-start.2 = (f32[2,256,128]{2,1,0:T(8,128)S(1)}, f32[2,256,128]{2,1,0:T(8,128)}, u32[]{:S(2)}) copy-start(f32[2,256,128]{2,1,0:T(8,128)} %constant.20.clone.inverse_hbm.inverse_ref) | copy-start | bytes 786436
  41.1 28.8 %copy-start.3 = (bf16[2,3,128,128]{3,2,1,0:T(8,128)(2,1)S(1)}, bf16[2,3,128,128]{3,2,1,0:T(8,128)(2,1)}, u32[]{:S(2)}) copy-start(bf16[2,3,128,128]{3,2,1,0:T(8,128)(2,1)} %constant.26.clone.basis_ref) | copy-start | bytes 589828
  41.1 28.8 %copy-start.4 = (bf16[2,3,128,128]{3,2,1,0:T(8,128)(2,1)S(1)}, bf16[2,3,128,128]{3,2,1,0:T(8,128)(2,1)}, u32[]{:S(2)}) copy-start(bf16[2,3,128,128]{3,2,1,0:T(8,128)(2,1)} %constant.25.clone.links_ref) | copy-start | bytes 589828

commit v2 on v1

v2 whole, which is shorter than its diff:
```python
import functools

import jax
import jax.numpy as jnp
import numpy as np
from jax import lax
from jax.experimental import pallas as pl
from jax.experimental.pallas import tpu as pltpu
from jax.sharding import PartitionSpec as P

NEWTON = 4
ROWS = ("grp", "px")
EVERY = ("grp", "px", "py")
GROUP = 2
VMEM_BYTES = 48 * 1024 * 1024
DIRECT = ((1,), (0,))
CROSS = ((1,), (1,))


def table_parts(table, count):
    rest = np.asarray(table, np.float32)
    parts = []
    for _ in range(count):
        parts.append(rest.astype(jnp.bfloat16))
        rest = rest - parts[-1].astype(np.float32)
    return np.stack(parts)


def parts_of(value, count):
    parts = [value.astype(jnp.bfloat16)]
    for _ in range(count - 1):
        value = value - parts[-1].astype(jnp.float32)
        parts.append(value.astype(jnp.bfloat16))
    return parts


def orders(count):
    return [(i, order - i) for order in range(count - 1, -1, -1) for i in range(order + 1)]


def long_table(table, count, axis):
    parts = table_parts(table, count)
    return np.concatenate([parts[j] for _, j in orders(count)], axis=axis)


def long_data(value, count, axis):
    parts = parts_of(value, count)
    return jnp.concatenate([parts[i] for i, _ in orders(count)], axis=axis)


def wide_table(table, count):
    parts = table_parts(table, count)
    none = np.zeros_like(parts[0])
    if count == 2:
        grid = [(0, 1), (0, None)]
    else:
        grid = [(0, 1), (0, 1), (2, None), (0, None)]
    return np.block([[none if k is None else parts[k] for k in row] for row in grid])


def wide_product(value, table, count):
    parts = parts_of(value, count)
    data = parts if count == 2 else [parts[0], parts[1], parts[0], parts[2]]
    both = one_product(jnp.concatenate(data, axis=1), table, DIRECT)
    half = both.shape[1] // 2
    return both[:, :half] + both[:, half:]


def one_product(left, right, dims):
    return lax.dot_general(left, right, (dims, ((), ())), preferred_element_type=jnp.float32)


def squared_sines(length, period):
    return 4.0 * np.sin(np.pi * np.arange(length) / period) ** 2


def hartley_table(length):
    index = np.arange(length)
    angles = (index[:, None] * index[None, :] % length) * (2.0 * np.pi / length)
    return (np.cos(angles) + np.sin(angles)) / np.sqrt(length)


def elimination_table(levels, row_count, col_count, blocks, pieces, pair):
    eigen = squared_sines(col_count, col_count)[:, None] + squared_sines(row_count, row_count)
    factors = [1.0 / (1.0 + eigen)]
    for _ in range(levels // 2 - 1):
        factors.append(1.0 / (2.0 + eigen - factors[-1]))
    gap = 1.0 - factors[-1] ** 2
    middle = np.where(eigen > 0.0, 1.0 / np.where(eigen > 0.0, gap, 1.0), 0.0)
    table = np.stack(factors + [middle]).astype(np.float32)
    table = table.reshape(levels // 2 + 1, pieces, blocks, 1, -1, row_count).transpose(2, 0, 1, 3, 4, 5)
    table = np.broadcast_to(table, table.shape[:3] + (pair,) + table.shape[4:])
    return np.ascontiguousarray(table).reshape(blocks, levels // 2 + 1, -1, row_count)


def slots(here, rows, b, kind, index):
    if kind == "level":
        return b * rows + index
    if kind == "later":
        return (2 + b) * rows + index
    base = 4 * rows + b * (rows // 2)
    return base + (index - 1 if kind == "row" else here - 1 + index)


def interior_tables(here, rows, cols, last):
    pair = 2
    lanes = here * pair * rows
    inner = here - 1
    chain = 2.0 * np.eye(inner) - np.eye(inner, k=1) - np.eye(inner, k=-1)
    if last:
        chain[-1, -1] = 1.0
    time_values, time_basis = np.linalg.eigh(chain)
    row_index = np.arange(1, rows)
    row_basis = np.sqrt(2.0 / rows) * np.sin(np.pi * np.outer(row_index, row_index) / rows)
    row_values = squared_sines(rows, 2 * rows)
    col_values = squared_sines(cols, cols)
    basis = np.zeros((here, pair, rows, here, pair, rows))
    inverse = np.zeros((cols, here, pair, rows))
    linked = np.zeros((here, pair, rows, lanes))
    for b in range(pair):
        for k in range(1, here):
            for t in range(1, here):
                basis[t, b, 1:, k, b, 1:] = time_basis[t - 1, k - 1] * row_basis
            inverse[:, k, b, 1:] = 1.0 / (
                col_values[:, None] + time_values[k - 1] + row_values[None, 1:]
            )
        for x in range(1, rows):
            linked[1, b, x, slots(here, rows, b, "level", x)] = 1.0
            if not last:
                linked[here - 1, b, x, slots(here, rows, b, "later", x)] = 1.0
        for t in range(1, here):
            linked[t, b, 1, slots(here, rows, b, "row", t)] = 1.0
            linked[t, b, rows - 1, slots(here, rows, b, "next", t)] = 1.0
    basis = basis.reshape(lanes, lanes)
    linked = linked.reshape(lanes, lanes)
    inverse = inverse.reshape(cols, lanes)
    to_edges = basis.T @ linked
    from_edges = to_edges.T.copy()
    for b in range(pair):
        ones = np.zeros((here, pair, rows))
        ones[1:, b, 1:] = 1.0
        from_edges[slots(here, rows, b, "next", here)] = -(ones.reshape(-1) @ basis)
    return basis, inverse, to_edges, from_edges


def constant_source(here, rows, time_blocks, row_blocks, tables):
    levels, row_count = here * time_blocks, rows * row_blocks
    field = np.zeros((levels + 1, row_count))
    ones = np.zeros((here, 2, rows))
    ones[1:, 0, 1:] = 1.0
    for i in range(time_blocks):
        basis, inverse, to_edges, _ = tables[1 if i == time_blocks - 1 else 0]
        edge = ((ones.reshape(-1) @ basis) * inverse[0]) @ to_edges
        for j in range(row_blocks):
            t0, x0 = i * here, j * rows
            for x in range(rows):
                field[t0, x0 + x] += 1.0 + edge[slots(here, rows, 0, "level", x)]
                field[t0 + here, x0 + x] += edge[slots(here, rows, 0, "later", x)]
            for t in range(here):
                after = (x0 + rows) % row_count
                field[t0 + t, after] += edge[slots(here, rows, 0, "next", t)]
                if t > 0:
                    field[t0 + t, x0] += 1.0 + edge[slots(here, rows, 0, "row", t)]
    return field[:levels] @ hartley_table(row_count)


def exchange_pieces(blocks, width):
    count = len(blocks)
    lanes = count * width
    group = lax.broadcasted_iota(jnp.int32, blocks[0].shape, 1) // width
    step = 1
    while step < count:
        upper = (group // step) % 2 == 1
        fresh = list(blocks)
        for j in range(count):
            if (j // step) % 2 == 0:
                low, high = blocks[j], blocks[j + step]
                fresh[j] = jnp.where(upper, pltpu.roll(high, step * width, 1), low)
                fresh[j + step] = jnp.where(upper, high, pltpu.roll(low, lanes - step * width, 1))
        blocks = fresh
        step *= 2
    return blocks


def source_kernel(
    levels,
    pair,
    mult_ref,
    aux_ref,
    start_hbm,
    end_hbm,
    hart_hbm,
    basis_hbm,
    inverse_hbm,
    edges_hbm,
    out_ref,
    inner_ref,
    density_ref,
    hart_ref,
    basis_ref,
    inverse_ref,
    edges_ref,
    sems,
):
    _, here, batch, rows, cols = mult_ref.shape
    lanes = here * pair * rows
    pieces = lanes // rows
    each = cols // pieces
    first = lax.axis_index("py") * here
    last = (first + here == levels).astype(jnp.int32)
    starts = jnp.where(first == 0, 1.0, 0.0)
    ends = last.astype(jnp.float32)
    step = pl.program_id(0)

    def tables():
        return [
            pltpu.make_async_copy(hart_hbm, hart_ref, sems.at[2]),
            pltpu.make_async_copy(basis_hbm.at[last], basis_ref, sems.at[3]),
            pltpu.make_async_copy(inverse_hbm.at[last], inverse_ref, sems.at[4]),
            pltpu.make_async_copy(edges_hbm.at[last], edges_ref, sems.at[5]),
        ]

    @pl.when(step == 0)
    def _():
        copies = [
            pltpu.make_async_copy(start_hbm, density_ref.at[0], sems.at[0]),
            pltpu.make_async_copy(end_hbm, density_ref.at[1], sems.at[1]),
        ]
        for copy in copies + tables():
            copy.start()
        for copy in copies:
            copy.wait()

    row_index = lax.broadcasted_iota(jnp.int32, (rows, cols), 0)
    first_row = row_index == 0
    field = []
    for q in range(batch // pair):
        blocks = []
        earlier = [0.0] * pair
        rims = jnp.zeros((rows, cols), jnp.float32)
        for t in range(here):
            for b in range(pair):
                at = q * pair + b
                time = aux_ref[0, t, at] - mult_ref[0, t, at]
                if t == here - 1:
                    time = time * (1.0 - ends)
                along = aux_ref[1, t, at] - mult_ref[1, t, at]
                second = aux_ref[2, t, at] - mult_ref[2, t, at]
                beside = jnp.where(first_row, 0.0, pltpu.roll(along, 1, 0))
                total = (earlier[b] - time) + (beside - along)
                total = total + (pltpu.roll(second, 1, 1) - second)
                if t == 0:
                    total = total - density_ref[0, step * batch + at] * starts
                if t == here - 1:
                    total = total + density_ref[1, step * batch + at] * ends
                earlier[b] = time
                blocks.append(total)
                base = b * (rows // 2)
                if t > 0:
                    rims = jnp.where(row_index == base + t - 1, total[:1], rims)
                rims = jnp.where(row_index == base + here - 1 + t, along[rows - 1 :], rims)
        spare = jnp.zeros((lanes - (2 * pair + 1) * rows, cols), jnp.float32)
        nodes = jnp.concatenate(blocks + blocks[:pair] + earlier + [rims, spare], axis=0)
        field.append(long_data(nodes, 2, 1))

    @pl.when(step == 0)
    def _():
        for copy in tables():
            copy.wait()

    modes = [one_product(hart_ref[...], nodes, CROSS) for nodes in field]
    inner = [wide_product(mode[:, :lanes], basis_ref[...], 2) for mode in modes]
    gone = [wide_product(value * inverse_ref[...], edges_ref[...], 2) for value in inner]
    for q in range(batch // pair):
        inner_ref[q] = inner[q]
        edges = modes[q][:, lanes:] + gone[q]
        blocks = exchange_pieces([edges[j * each : (j + 1) * each] for j in range(pieces)], rows)
        for k in range(out_ref.shape[2]):
            out_ref[:, q, k] = blocks[k].reshape(out_ref.shape[0], out_ref.shape[3], lanes)


def solve_kernel(
    in_ref, hart_ref, back_ref, ones_ref, table_ref, out_ref, field_ref, mean_ref, factor_ref, rim_ref, sem
):
    row_blocks, time_blocks, kinds, few, lanes = in_ref.shape
    levels, high, cols = field_ref.shape
    here = levels // time_blocks
    rows = cols // row_blocks
    pieces = lanes // rows
    tall = (kinds - 1) * few
    count = high // tall
    half = levels // 2
    mine = lax.axis_index("grp") * lax.axis_size("px") + lax.axis_index("px")
    fetch = pltpu.make_async_copy(table_ref.at[mine], factor_ref, sem)
    fetch.start()
    stack = tall // few
    lane = lax.broadcasted_iota(jnp.int32, (tall, cols), 1) % rows
    row = lax.broadcasted_iota(jnp.int32, (tall, cols), 0)
    low = row < tall // 2
    even = (row // few) % 2 == 0

    def shift(value, steps):
        return pltpu.roll(value, steps % cols, 1)

    def swap(value):
        return pltpu.roll(value, tall // 2, 0)

    def offset(kind, t):
        return slots(here, rows, 0, kind, t) - 4 * rows

    def exchange(get):
        groups = [
            exchange_pieces([get(g * pieces + j) for j in range(pieces)], rows)
            for g in range(row_blocks // pieces)
        ]
        return [jnp.concatenate([group[k] for group in groups], axis=1) for k in range(pieces)]

    for h in range(time_blocks // stack):
        times = slice(h * stack, (h + 1) * stack)
        for j, rim in enumerate(exchange(lambda x: in_ref[x, times, kinds - 1].reshape(tall, lanes))):
            rim_ref[h, j, 0] = rim
            rim_ref[h, j, 1] = shift(rim, -(rows // 2))

    def forward(i, carry):
        main = exchange(lambda x: in_ref[x, i, : kinds - 1].reshape(tall, lanes))
        here_rows = slice(i % stack * few, (i % stack + 1) * few)
        field = [[] for _ in range(here)]
        later = []
        for q in range(count):
            one, two = main[2 * q], main[2 * q + 1]
            level = jnp.where(low, one, swap(two)) + carry[q]
            later.append(jnp.where(low, swap(one), two))
            rim = jnp.concatenate(
                [rim_ref[i // stack, 2 * q + j, b, here_rows] for j in range(2) for b in range(2)],
                axis=0,
            )
            for t in range(here):
                value = shift(rim, rows - offset("next", t))
                if t > 0:
                    value = value + shift(rim, -offset("row", t))
                value = jnp.where(lane == 0, value, 0.0)
                field[t].append(value + level if t == 0 else value)
        field = jnp.concatenate(sum(field, []), axis=0)
        modes = one_product(long_data(field, 2, 1), hart_ref[...], DIRECT)
        field_ref[pl.ds(i * here, here)] = modes.reshape(here, high, cols)
        return tuple(later)

    blank = jnp.zeros((tall, cols), jnp.float32)
    carry = (blank,) * count
    for i in range(time_blocks):
        carry = forward(i, carry)
    fetch.wait()

    mean_ref[...] = jnp.zeros(mean_ref.shape, jnp.float32)

    @pl.when(mine == 0)
    def _():
        shape = (tall, 128)
        spot = lax.broadcasted_iota(jnp.int32, shape, 0)
        zero = (spot % few == 0) & (spot < tall // 2)
        zero = zero & (lax.broadcasted_iota(jnp.int32, shape, 1) == 0)
        scale = float(np.sqrt(cols)) / (levels * cols)
        sums = field_ref[0, :tall, :128]
        for t in range(1, levels):
            sums = sums + field_ref[t, :tall, :128]
        mean = jnp.sum(jnp.where(zero, sums * scale, 0.0), axis=1, keepdims=True)
        mean_ref[0] = jnp.broadcast_to(mean, (tall, cols))
        for t in range(levels):
            field_ref[t, :tall] = field_ref[t, :tall] - mean * ones_ref[t : t + 1]

    left = jnp.zeros(field_ref.shape[1:], jnp.float32)
    right = left
    for t in range(half):
        factor = factor_ref[t]
        left = (field_ref[t] + left) * factor
        right = (field_ref[levels - 1 - t] + right) * factor
        if t < half - 1:
            field_ref[t] = left
            field_ref[levels - 1 - t] = right
    first = (left + factor * right) * factor_ref[half]
    right = right + factor * first
    left = first
    field_ref[half - 1] = left
    field_ref[half] = right
    for t in range(half - 2, -1, -1):
        factor = factor_ref[t]
        left = field_ref[t] + factor * left
        right = field_ref[levels - 1 - t] + factor * right
        field_ref[t] = left
        field_ref[levels - 1 - t] = right

    def backward(i, carry):
        here_rows = slice(i % stack * few, (i % stack + 1) * few)
        field = field_ref[pl.ds(i * here, here)].reshape(here * high, cols)
        values = one_product(long_data(field, 3, 1), back_ref[...], DIRECT)
        main, first = [], []
        for q in range(count):
            part = [values[t * high + q * tall : t * high + (q + 1) * tall] for t in range(here)]
            rim = jnp.where(lane == offset("next", here), mean_ref[q], 0.0)
            for t in range(here):
                at = offset("next", t)
                rim = jnp.where(lane == at, shift(part[t], at - rows), rim)
                if t > 0:
                    at = offset("row", t)
                    rim = jnp.where(lane == at, shift(part[t], at), rim)
            rim = jnp.where(even, rim, shift(rim, rows // 2))
            rim = rim + pltpu.roll(rim, tall - few, 0)
            rim_ref[i // stack, 2 * q, 0, here_rows] = rim[:few]
            rim_ref[i // stack, 2 * q + 1, 0, here_rows] = rim[tall // 2 : tall // 2 + few]
            main.append(jnp.where(low, part[0], swap(carry[q])))
            main.append(jnp.where(low, swap(part[0]), carry[q]))
            first.append(part[0])
        for g in range(row_blocks // pieces):
            cut = slice(g * lanes, (g + 1) * lanes)
            for j, value in enumerate(exchange_pieces([a[:, cut] for a in main], rows)):
                out_ref[g * pieces + j, i, : kinds - 1] = value.reshape(kinds - 1, few, lanes)
        return tuple(first)

    carry = (blank,) * count
    for i in range(time_blocks - 1, -1, -1):
        carry = backward(i, carry)
    for h in range(time_blocks // stack):
        times = slice(h * stack, (h + 1) * stack)
        for g in range(row_blocks // pieces):
            cut = slice(g * lanes, (g + 1) * lanes)
            rims = exchange_pieces([rim_ref[h, j, 0, :, cut] for j in range(pieces)], rows)
            for j, value in enumerate(rims):
                out_ref[g * pieces + j, times, kinds - 1] = value.reshape(stack, few, lanes)


def step_kernel(
    levels,
    pair,
    mult_ref,
    edge_ref,
    inner_ref,
    hart_ref,
    links_ref,
    inverse_ref,
    basis_ref,
    mult_out,
    aux_out,
):
    _, here, batch, rows, cols = mult_ref.shape
    lanes = here * pair * rows
    pieces = lanes // rows
    kinds = edge_ref.shape[2]
    first = lax.axis_index("py") * here
    last = (first + here == levels).astype(jnp.int32)
    inside = 1.0 - last.astype(jnp.float32)
    row_index = lax.broadcasted_iota(jnp.int32, (rows, cols), 0)
    edges = []
    for q in range(batch // pair):
        blocks = [edge_ref[:, q, k].reshape(cols // pieces, lanes) for k in range(kinds)]
        blocks += [jnp.zeros((cols // pieces, lanes), jnp.float32)] * (pieces - kinds)
        edges.append(jnp.concatenate(exchange_pieces(blocks, rows), axis=0))
    linked = [wide_product(edge, links_ref[last], 3) for edge in edges]
    gone = [(inner_ref[q] + linked[q]) * inverse_ref[last] for q in range(batch // pair)]
    nodes = [wide_product(value, basis_ref[last], 3) for value in gone]
    whole = [jnp.concatenate(both, axis=1).T[: lanes + kinds * rows] for both in zip(nodes, edges)]
    potential = [one_product(long_data(value, 3, 1), hart_ref[...], DIRECT) for value in whole]
    for q in range(batch // pair):
        step_part(q, pair, potential[q], inside, row_index, mult_ref, mult_out, aux_out)


def step_part(q, pair, values, inside, row_index, mult_ref, mult_out, aux_out):
    _, here, _, rows, cols = mult_ref.shape
    lanes = here * pair * rows

    def piece(start, count):
        return values[start : start + count]

    rims = lanes + 4 * rows
    phi = []
    for t in range(here):
        for b in range(pair):
            if t == 0:
                phi.append(piece(lanes + b * rows, rows))
            else:
                row = piece(lanes + slots(here, rows, b, "row", t), 1)
                phi.append(jnp.where(row_index == 0, row, piece((t * pair + b) * rows, rows)))
    for b in range(pair):
        phi.append(piece(lanes + (pair + b) * rows, rows))
    for t in range(here):
        for b in range(pair):
            mine = phi[t * pair + b]
            time_rate = phi[(t + 1) * pair + b] - mine
            if t == here - 1:
                time_rate = time_rate * inside
            row = piece(lanes + slots(here, rows, b, "next", t), 1)
            below = jnp.where(row_index == rows - 1, row, pltpu.roll(mine, rows - 1, 0))
            gradient = (time_rate, below - mine, pltpu.roll(mine, cols - 1, 1) - mine)
            mult = [mult_ref[c, t, q * pair + b] for c in range(3)]
            time_part, one, two = (g + m for g, m in zip(gradient, mult))
            kinetic = 0.5 * (one * one + two * two)
            center = 1.0 + time_part
            scaling = jnp.maximum(center, 1.0) + jnp.exp(jnp.log(kinetic) * (1.0 / 3.0))
            twice = center + center
            for _ in range(NEWTON):
                residue = scaling * scaling * (scaling - center) - kinetic
                derivative = scaling * (3.0 * scaling - twice)
                change = residue * pl.reciprocal(derivative, approx=True)
                scaling = jnp.maximum(scaling - change, 1.0)
            feasible = time_part + kinetic <= 0.0
            shrink = jnp.where(feasible, 1.0, 1.0 / scaling)
            fresh = (
                jnp.where(feasible, time_part, time_part - (scaling - 1.0)),
                one * shrink,
                two * shrink,
            )
            for c in range(3):
                aux_out[c, t, q * pair + b] = fresh[c]
                mult_out[c, t, q * pair + b] = mult[c] + (gradient[c] - fresh[c])


def params(size=48):
    return pltpu.CompilerParams(vmem_limit_bytes=size * 1024 * 1024)


def whole_block(array):
    return pl.BlockSpec(array.shape, lambda p: (0,) * array.ndim)


def local(multiplier, auxiliary, density_start, density_end):
    _, here, batch, rows, cols = multiplier.shape
    time_blocks = lax.axis_size("py")
    row_blocks = lax.axis_size("grp") * lax.axis_size("px")
    levels = here * time_blocks
    row_count = rows * row_blocks
    pair = batch // time_blocks
    lanes = here * pair * rows
    pieces = lanes // rows
    kinds = 2 * pair + 1
    few = cols // (pieces * row_blocks)
    both = [interior_tables(here, rows, cols, last) for last in (False, True)]
    hart_there = long_table(hartley_table(cols), 2, 1)
    hart_back = long_table(hartley_table(cols), 3, 0)
    rows_there = long_table(hartley_table(row_count), 2, 0)
    rows_back = long_table(hartley_table(row_count), 3, 0)
    basis2 = np.stack([wide_table(one[0], 2) for one in both])
    basis3 = np.stack([wide_table(one[0].T, 3) for one in both])
    inverse = np.stack([one[1] for one in both]).astype(np.float32)
    to_edges = np.stack([wide_table(one[2], 2) for one in both])
    from_edges = np.stack([wide_table(one[3], 3) for one in both])
    ones = constant_source(here, rows, time_blocks, row_blocks, both).astype(np.float32)
    factors = elimination_table(levels, row_count, cols, row_blocks, pieces, pair)

    group = GROUP
    five = pl.BlockSpec((3, here, pair * group, rows, cols), lambda p: (0, 0, p, 0, 0))
    chunks = pl.BlockSpec((row_blocks, group, kinds, few, lanes), lambda p: (0, p, 0, 0, 0))
    away = pl.BlockSpec(memory_space=pltpu.HBM)
    chunked = jax.ShapeDtypeStruct((row_blocks, time_blocks, kinds, few, lanes), jnp.float32)
    kept = pl.BlockSpec((group, cols, lanes), lambda p: (p, 0, 0))
    edges, inner = pl.pallas_call(
        functools.partial(source_kernel, levels, pair),
        grid=(time_blocks // group,),
        in_specs=[five, five] + [away] * 6,
        out_specs=[chunks, kept],
        out_shape=[chunked, jax.ShapeDtypeStruct((time_blocks, cols, lanes), jnp.float32)],
        scratch_shapes=[
            pltpu.VMEM((2,) + density_start.shape, jnp.float32),
            pltpu.VMEM(hart_there.shape, jnp.bfloat16),
            pltpu.VMEM(basis2.shape[1:], jnp.bfloat16),
            pltpu.VMEM(inverse.shape[1:], jnp.float32),
            pltpu.VMEM(to_edges.shape[1:], jnp.bfloat16),
            pltpu.SemaphoreType.DMA((6,)),
        ],
        compiler_params=params(56),
        name="source",
    )(multiplier, auxiliary, density_start, density_end, hart_there, basis2, inverse, to_edges)

    def spread(value):
        flat = value.reshape((row_blocks * time_blocks,) + value.shape[2:])
        return lax.all_to_all(flat, EVERY, 0, 0, tiled=True).reshape(value.shape)

    vmem = pl.BlockSpec(memory_space=pltpu.VMEM)
    solved = pl.pallas_call(
        solve_kernel,
        in_specs=[vmem, vmem, vmem, vmem, pl.BlockSpec(memory_space=pl.ANY)],
        out_specs=vmem,
        out_shape=chunked,
        scratch_shapes=[
            pltpu.VMEM((levels, pair * pieces * few, row_count), jnp.float32),
            pltpu.VMEM((pieces // 2, 2 * pair * few, row_count), jnp.float32),
            pltpu.VMEM(factors.shape[1:], jnp.float32),
            pltpu.VMEM((time_blocks // (2 * pair), pieces, 2, 2 * pair * few, row_count), jnp.float32),
            pltpu.SemaphoreType.DMA,
        ],
        compiler_params=params(),
        name="solve",
    )(spread(edges), rows_there, rows_back, ones, factors)

    result = jax.ShapeDtypeStruct(multiplier.shape, jnp.float32)
    mult_next, aux_next = pl.pallas_call(
        functools.partial(step_kernel, levels, pair),
        grid=(time_blocks // group,),
        in_specs=[five, chunks, kept]
        + [whole_block(a) for a in (hart_back, from_edges, inverse, basis3)],
        out_specs=[five, five],
        out_shape=[result, result],
        compiler_params=params(),
        name="step",
    )(multiplier, spread(solved), inner, hart_back, from_edges, inverse, basis3)
    return mult_next, aux_next


def solution(mesh):
    field = P(None, "py", None, ROWS, None)
    density = P(None, ROWS, None)
    return jax.shard_map(
        local,
        mesh=mesh,
        in_specs=(field, field, density, density),
        out_specs=(field, field),
        check_vma=False,
    )
```

time: 84 us -> 71.3 us (0.85)
  blocking collectives: 54.3 us -> 46.1 us
  Pallas kernels: 28.5 us -> 24.1 us
    all_to_all x2, blocking collectives: 54.3 us -> 46.1 us  [spread(): return lax.all_to_all(flat, EVERY, 0, 0, tiled=True).reshape(value.shape)]
    pallas_call x1, Pallas kernels: 13.7 us -> 10.7 us  [local(): pl.pallas_call(functools.partial(step_kernel, levels, pair), grid=(time_b...]
    pallas_call x1, Pallas kernels: 9.5 us -> 8.4 us  [local(): pl.pallas_call(functools.partial(source_kernel, levels, pair), grid=(time...]
where the time goes in v2:
time: 71.3 us; the launch traced here: 71 us
  blocking collectives  46.1 us (65%)
  Pallas kernels  24.1 us (34%)
  between operations  0.72 us (1%)
    all_to_all x2, blocking collectives, spread(): return lax.all_to_all(flat, EVERY, 0, 0, tiled=True).reshape(value.shape)  46.1 us
    pallas_call x1, Pallas kernels, local(): pl.pallas_call(functools.partial(step_kernel, levels, pair), grid=(time_b...  10.7 us
    pallas_call x1, Pallas kernels, local(): pl.pallas_call(functools.partial(source_kernel, levels, pair), grid=(time...  8.4 us
    pallas_call x1, Pallas kernels, local(): pl.pallas_call(solve_kernel, in_specs=[vmem, vmem, vmem, vmem, pl.BlockSp...  5.05 us

profile of v2, /device:TPU:1, one launch (start us, length us, event | category | flops | bytes accessed | tf_op | source)
XLA Modules:
  0.0 71.0 jit_solution(17587128936814519457)
XLA Ops:
  0.6 0.0 copy-start
  0.6 0.0 copy-start.5
  0.7 0.0 copy-start.6
  0.7 8.4 %source.1 = (f32[16,8,5,2,128]{4,3,2,1,0:T(2,128)}, f32[8,256,128]{2,1,0:T(8,128)}) custom-call(f32[3,4,16,16,256]{4,3,2,1,0:T(8,128)} %mult_ref.3, f32[3,4,16,16,256]{4,3,2,1,0:T(8,128)} %aux_ref.1, f32[16,16,256]{2,1,0:T(8,128)} %start_hbm.1, f32[16,16,256]{2,1,0:T(8,128)} %end_hbm.1, bf16[256,768]{1,0:T(8,128)(2,1)} %constant.20.clone.hart_hbm, ...), custom_call_target="tpu_custom_call" | custom-call | tf_op jit(solution)/shard_map/source/pallas_call | solution.py:554
  9.1 26.7 %all_to_all.10 = f32[128,5,2,128]{3,2,1,0:T(2,128)S(1)} all-to-all(f32[128,5,2,128]{3,2,1,0:T(2,128)} %bitcast.7), channel_id=1, replica_groups=mesh['grp'=2,'px'=8,'py'=8] {'grp','px','py'}, dimensions={0} | all-to-all | bytes 1310720 | tf_op jit(solution)/shard_map/all_to_all | solution.py:574
  35.8 0.0 copy-done
  35.8 0.0 copy-done.5
  35.8 0.0 copy-done.6
  35.8 0.0 copy-start.1
  35.8 0.0 copy-start.2
  35.9 0.0 copy-start.3
  35.9 0.0 copy-start.4
  35.9 5.0 %solve.1 = f32[16,8,5,2,128]{4,3,2,1,0:T(2,128)S(1)} custom-call(f32[16,8,5,2,128]{4,3,2,1,0:T(2,128)S(1)} %bitcast.4, bf16[768,256]{1,0:T(8,128)(2,1)S(1)} %copy-done.5, bf16[1536,256]{1,0:T(8,128)(2,1)S(1)} %copy-done, f32[32,256]{1,0:T(8,128)S(1)} %copy-done.6, f32[16,17,32,256]{3,2,1,0:T(8,128)} %constant.27.clone.table_ref), custom_call_target="tpu_custom_call" | custom-call | tf_op jit(solution)/shard_map/solve/pallas_call | solution.py:577
  40.9 19.3 %all_to_all.11 = f32[128,5,2,128]{3,2,1,0:T(2,128)S(1)} all-to-all(f32[128,5,2,128]{3,2,1,0:T(2,128)S(1)} %bitcast.5), channel_id=1, replica_groups=mesh['grp'=2,'px'=8,'py'=8] {'grp','px','py'}, dimensions={0} | all-to-all | bytes 1310720 | tf_op jit(solution)/shard_map/all_to_all | solution.py:574
  60.3 0.0 copy-done.1
  60.3 0.0 copy-done.2
  60.3 0.0 copy-done.3
  60.3 0.0 copy-done.4
  60.3 10.7 %step.1 = (f32[3,4,16,16,256]{4,3,2,1,0:T(8,128)}, f32[3,4,16,16,256]{4,3,2,1,0:T(8,128)}) custom-call(f32[3,4,16,16,256]{4,3,2,1,0:T(8,128)} %mult_ref.3, f32[16,8,5,2,128]{4,3,2,1,0:T(2,128)S(1)} %bitcast.6, f32[8,256,128]{2,1,0:T(8,128)S(1)} %copy-done.1, bf16[1536,256]{1,0:T(8,128)(2,1)S(1)} %copy-done, bf16[2,512,256]{2,1,0:T(8,128)(2,1)S(1)} %copy-done.4, ...), custom_call_target="tpu_custom_call" | custom-call | tf_op jit(solution)/shard_map/step/pallas_call | solution.py:594
Async XLA Ops:
  0.6 35.2 %copy-start = (bf16[1536,256]{1,0:T(8,128)(2,1)S(1)}, bf16[1536,256]{1,0:T(8,128)(2,1)}, u32[]{:S(2)}) copy-start(bf16[1536,256]{1,0:T(8,128)(2,1)} %constant.25.clone.back_ref.hart_ref) | copy-start | bytes 2359300
  0.6 35.2 %copy-start.5 = (bf16[768,256]{1,0:T(8,128)(2,1)S(1)}, bf16[768,256]{1,0:T(8,128)(2,1)}, u32[]{:S(2)}) copy-start(bf16[768,256]{1,0:T(8,128)(2,1)} %constant.24.clone.hart_ref) | copy-start | bytes 1179652
  0.7 35.2 %copy-start.6 = (f32[32,256]{1,0:T(8,128)S(1)}, f32[32,256]{1,0:T(8,128)}, u32[]{:S(2)}) copy-start(f32[32,256]{1,0:T(8,128)} %constant.26.clone.ones_ref) | copy-start | bytes 98308
  35.8 24.5 %copy-start.1 = (f32[8,256,128]{2,1,0:T(8,128)S(1)}, f32[8,256,128]{2,1,0:T(8,128)}, u32[]{:S(2)}) copy-start(f32[8,256,128]{2,1,0:T(8,128)} %get-tuple-element.5.inner_ref) | copy-start | bytes 3145732
  35.8 24.4 %copy-start.2 = (f32[2,256,128]{2,1,0:T(8,128)S(1)}, f32[2,256,128]{2,1,0:T(8,128)}, u32[]{:S(2)}) copy-start(f32[2,256,128]{2,1,0:T(8,128)} %constant.22.clone.inverse_hbm.inverse_ref) | copy-start | bytes 786436
  35.9 24.4 %copy-start.3 = (bf16[2,512,256]{2,1,0:T(8,128)(2,1)S(1)}, bf16[2,512,256]{2,1,0:T(8,128)(2,1)}, u32[]{:S(2)}) copy-start(bf16[2,512,256]{2,1,0:T(8,128)(2,1)} %constant.29.clone.basis_ref) | copy-start | bytes 1572868
  35.9 24.4 %copy-start.4 = (bf16[2,512,256]{2,1,0:T(8,128)(2,1)S(1)}, bf16[2,512,256]{2,1,0:T(8,128)(2,1)}, u32[]{:S(2)}) copy-start(bf16[2,512,256]{2,1,0:T(8,128)(2,1)} %constant.28.clone.links_ref) | copy-start | bytes 1572868

commit v3 on v2

--- a/solution.py
+++ b/solution.py
@@ -11,7 +11,8 @@
 NEWTON = 4
 ROWS = ("grp", "px")
 EVERY = ("grp", "px", "py")
-GROUP = 2
+PARTS = 2
+STEP_PARTS = 2
 VMEM_BYTES = 48 * 1024 * 1024
 DIRECT = ((1,), (0,))
 CROSS = ((1,), (1,))
@@ -185,98 +186,122 @@
 def source_kernel(
     levels,
     pair,
-    mult_ref,
-    aux_ref,
+    mult_hbm,
+    aux_hbm,
     start_hbm,
     end_hbm,
     hart_hbm,
     basis_hbm,
     inverse_hbm,
     edges_hbm,
-    out_ref,
-    inner_ref,
+    out_hbm,
+    inner_hbm,
+    mult_ref,
+    aux_ref,
     density_ref,
     hart_ref,
     basis_ref,
     inverse_ref,
     edges_ref,
-    sems,
+    out_ref,
+    inner_ref,
+    field_sems,
+    table_sems,
+    out_sems,
 ):
     _, here, batch, rows, cols = mult_ref.shape
     lanes = here * pair * rows
     pieces = lanes // rows
     each = cols // pieces
+    total_pairs = batch // pair
     first = lax.axis_index("py") * here
-    last = (first + here == levels).astype(jnp.int32)
-    starts = jnp.where(first == 0, 1.0, 0.0)
-    ends = last.astype(jnp.float32)
-    step = pl.program_id(0)
-
-    def tables():
-        return [
-            pltpu.make_async_copy(hart_hbm, hart_ref, sems.at[2]),
-            pltpu.make_async_copy(basis_hbm.at[last], basis_ref, sems.at[3]),
-            pltpu.make_async_copy(inverse_hbm.at[last], inverse_ref, sems.at[4]),
-            pltpu.make_async_copy(edges_hbm.at[last], edges_ref, sems.at[5]),
-        ]
-
-    @pl.when(step == 0)
-    def _():
-        copies = [
-            pltpu.make_async_copy(start_hbm, density_ref.at[0], sems.at[0]),
-            pltpu.make_async_copy(end_hbm, density_ref.at[1], sems.at[1]),
-        ]
-        for copy in copies + tables():
-            copy.start()
-        for copy in copies:
-            copy.wait()
+    at_start = first == 0
+    at_end = first + here == levels
+    last = at_end.astype(jnp.int32)
+    fields = []
+    for part in range(PARTS):
+        cut = pl.ds(part * batch // PARTS, batch // PARTS)
+        fields.append(
+            [
+                pltpu.make_async_copy(
+                    one.at[:, :, cut], other.at[:, :, cut], field_sems.at[n, part]
+                )
+                for n, (one, other) in enumerate(((mult_hbm, mult_ref), (aux_hbm, aux_ref)))
+            ]
+        )
+    tables = [
+        pltpu.make_async_copy(hart_hbm, hart_ref, table_sems.at[0]),
+        pltpu.make_async_copy(basis_hbm.at[last], basis_ref, table_sems.at[1]),
+        pltpu.make_async_copy(inverse_hbm.at[last], inverse_ref, table_sems.at[2]),
+        pltpu.make_async_copy(edges_hbm.at[last], edges_ref, table_sems.at[3]),
+    ]
+    start_copy = pltpu.make_async_copy(start_hbm, density_ref.at[0], table_sems.at[4])
+    end_copy = pltpu.make_async_copy(end_hbm, density_ref.at[1], table_sems.at[5])
+    for copy in fields[0] + tables + [start_copy, end_copy] + sum(fields[1:], []):
+        copy.start()
 
     row_index = lax.broadcasted_iota(jnp.int32, (rows, cols), 0)
     first_row = row_index == 0
-    field = []
-    for q in range(batch // pair):
-        blocks = []
-        earlier = [0.0] * pair
-        rims = jnp.zeros((rows, cols), jnp.float32)
-        for t in range(here):
-            for b in range(pair):
-                at = q * pair + b
-                time = aux_ref[0, t, at] - mult_ref[0, t, at]
-                if t == here - 1:
-                    time = time * (1.0 - ends)
-                along = aux_ref[1, t, at] - mult_ref[1, t, at]
-                second = aux_ref[2, t, at] - mult_ref[2, t, at]
-                beside = jnp.where(first_row, 0.0, pltpu.roll(along, 1, 0))
-                total = (earlier[b] - time) + (beside - along)
-                total = total + (pltpu.roll(second, 1, 1) - second)
-                if t == 0:
-                    total = total - density_ref[0, step * batch + at] * starts
-                if t == here - 1:
-                    total = total + density_ref[1, step * batch + at] * ends
-                earlier[b] = time
-                blocks.append(total)
-                base = b * (rows // 2)
-                if t > 0:
-                    rims = jnp.where(row_index == base + t - 1, total[:1], rims)
-                rims = jnp.where(row_index == base + here - 1 + t, along[rows - 1 :], rims)
-        spare = jnp.zeros((lanes - (2 * pair + 1) * rows, cols), jnp.float32)
-        nodes = jnp.concatenate(blocks + blocks[:pair] + earlier + [rims, spare], axis=0)
-        field.append(long_data(nodes, 2, 1))
-
-    @pl.when(step == 0)
-    def _():
-        for copy in tables():
+    outs = []
+    for part in range(PARTS):
+        for copy in fields[part]:
             copy.wait()
-
-    modes = [one_product(hart_ref[...], nodes, CROSS) for nodes in field]
-    inner = [wide_product(mode[:, :lanes], basis_ref[...], 2) for mode in modes]
-    gone = [wide_product(value * inverse_ref[...], edges_ref[...], 2) for value in inner]
-    for q in range(batch // pair):
-        inner_ref[q] = inner[q]
-        edges = modes[q][:, lanes:] + gone[q]
-        blocks = exchange_pieces([edges[j * each : (j + 1) * each] for j in range(pieces)], rows)
-        for k in range(out_ref.shape[2]):
-            out_ref[:, q, k] = blocks[k].reshape(out_ref.shape[0], out_ref.shape[3], lanes)
+        if part == 0:
+            start_copy.wait()
+            end_copy.wait()
+        mine = range(part * total_pairs // PARTS, (part + 1) * total_pairs // PARTS)
+        field = []
+        for q in mine:
+            blocks = []
+            earlier = [0.0] * pair
+            rims = jnp.zeros((rows, cols), jnp.float32)
+            for t in range(here):
+                for b in range(pair):
+                    at = q * pair + b
+                    time = aux_ref[0, t, at] - mult_ref[0, t, at]
+                    if t == here - 1:
+                        time = jnp.where(at_end, 0.0, time)
+                    along = aux_ref[1, t, at] - mult_ref[1, t, at]
+                    second = aux_ref[2, t, at] - mult_ref[2, t, at]
+                    beside = jnp.where(first_row, 0.0, pltpu.roll(along, 1, 0))
+                    total = (earlier[b] - time) + (beside - along)
+                    total = total + (pltpu.roll(second, 1, 1) - second)
+                    if t == 0:
+                        total = total - jnp.where(at_start, density_ref[0, at], 0.0)
+                    if t == here - 1:
+                        total = total + jnp.where(at_end, density_ref[1, at], 0.0)
+                    earlier[b] = time
+                    blocks.append(total)
+                    base = b * (rows // 2)
+                    if t > 0:
+                        rims = jnp.where(row_index == base + t - 1, total[:1], rims)
+                    rims = jnp.where(row_index == base + here - 1 + t, along[rows - 1 :], rims)
+            spare = jnp.zeros((lanes - (2 * pair + 1) * rows, cols), jnp.float32)
+            nodes = jnp.concatenate(blocks + blocks[:pair] + earlier + [rims, spare], axis=0)
+            field.append(long_data(nodes, 2, 1))
+        if part == 0:
+            for copy in tables:
+                copy.wait()
+        modes = [one_product(hart_ref[...], nodes, CROSS) for nodes in field]
+        inner = [wide_product(mode[:, :lanes], basis_ref[...], 2) for mode in modes]
+        gone = [wide_product(value * inverse_ref[...], edges_ref[...], 2) for value in inner]
+        for n, q in enumerate(mine):
+            inner_ref[q] = inner[n]
+            edges = modes[n][:, lanes:] + gone[n]
+            blocks = exchange_pieces(
+                [edges[j * each : (j + 1) * each] for j in range(pieces)], rows
+            )
+            for k in range(out_ref.shape[2]):
+                out_ref[:, q, k] = blocks[k].reshape(out_ref.shape[0], out_ref.shape[3], lanes)
+        cut = pl.ds(mine[0], len(mine))
+        outs += [
+            pltpu.make_async_copy(out_ref.at[:, cut], out_hbm.at[:, cut], out_sems.at[0, part]),
+            pltpu.make_async_copy(inner_ref.at[cut], inner_hbm.at[cut], out_sems.at[1, part]),
+        ]
+        for copy in outs[-2:]:
+            copy.start()
+    for copy in outs:
+        copy.wait()
 
 
 def solve_kernel(
@@ -431,94 +456,121 @@
 def step_kernel(
     levels,
     pair,
-    mult_ref,
+    mult_in,
     edge_ref,
     inner_ref,
     hart_ref,
     links_ref,
     inverse_ref,
     basis_ref,
+    mult_hbm,
+    aux_hbm,
+    mult_ref,
     mult_out,
     aux_out,
+    sems,
 ):
     _, here, batch, rows, cols = mult_ref.shape
     lanes = here * pair * rows
     pieces = lanes // rows
     kinds = edge_ref.shape[2]
+    total_pairs = batch // pair
     first = lax.axis_index("py") * here
     last = (first + here == levels).astype(jnp.int32)
     inside = 1.0 - last.astype(jnp.float32)
-    row_index = lax.broadcasted_iota(jnp.int32, (rows, cols), 0)
-    edges = []
-    for q in range(batch // pair):
-        blocks = [edge_ref[:, q, k].reshape(cols // pieces, lanes) for k in range(kinds)]
-        blocks += [jnp.zeros((cols // pieces, lanes), jnp.float32)] * (pieces - kinds)
-        edges.append(jnp.concatenate(exchange_pieces(blocks, rows), axis=0))
-    linked = [wide_product(edge, links_ref[last], 3) for edge in edges]
-    gone = [(inner_ref[q] + linked[q]) * inverse_ref[last] for q in range(batch // pair)]
-    nodes = [wide_product(value, basis_ref[last], 3) for value in gone]
-    whole = [jnp.concatenate(both, axis=1).T[: lanes + kinds * rows] for both in zip(nodes, edges)]
-    potential = [one_product(long_data(value, 3, 1), hart_ref[...], DIRECT) for value in whole]
-    for q in range(batch // pair):
-        step_part(q, pair, potential[q], inside, row_index, mult_ref, mult_out, aux_out)
-
-
-def step_part(q, pair, values, inside, row_index, mult_ref, mult_out, aux_out):
+    outs = []
+    fetches = []
+    for q in range(total_pairs):
+        cut = pl.ds(q * pair, pair)
+        fetches.append(
+            pltpu.make_async_copy(mult_in.at[:, :, cut], mult_ref.at[:, :, cut], sems.at[2, q])
+        )
+        fetches[q].start()
+    for part in range(STEP_PARTS):
+        mine = range(part * total_pairs // STEP_PARTS, (part + 1) * total_pairs // STEP_PARTS)
+        edges = []
+        for q in mine:
+            blocks = [edge_ref[:, q, k].reshape(cols // pieces, lanes) for k in range(kinds)]
+            blocks += [jnp.zeros((cols // pieces, lanes), jnp.float32)] * (pieces - kinds)
+            edges.append(jnp.concatenate(exchange_pieces(blocks, rows), axis=0))
+        linked = [wide_product(edge, links_ref[last], 3) for edge in edges]
+        gone = [(inner_ref[q] + link) * inverse_ref[last] for q, link in zip(mine, linked)]
+        nodes = [wide_product(value, basis_ref[last], 3) for value in gone]
+        whole = [
+            jnp.concatenate(both, axis=1).T[: lanes + kinds * rows] for both in zip(nodes, edges)
+        ]
+        potential = [one_product(long_data(value, 3, 1), hart_ref[...], DIRECT) for value in whole]
+        for q, values in zip(mine, potential):
+            fetches[q].wait()
+            step_part(q, pair, values, inside, mult_ref, mult_out, aux_out)
+            cut = pl.ds(q * pair, pair)
+            for n, (one, other) in enumerate(((mult_out, mult_hbm), (aux_out, aux_hbm))):
+                copy = pltpu.make_async_copy(one.at[:, :, cut], other.at[:, :, cut], sems.at[n, q])
+                copy.start()
+                outs.append(copy)
+    for copy in outs:
+        copy.wait()
+
+
+def step_part(q, pair, values, inside, mult_ref, mult_out, aux_out):
     _, here, _, rows, cols = mult_ref.shape
     lanes = here * pair * rows
-
-    def piece(start, count):
-        return values[start : start + count]
-
-    rims = lanes + 4 * rows
-    phi = []
-    for t in range(here):
-        for b in range(pair):
-            if t == 0:
-                phi.append(piece(lanes + b * rows, rows))
-            else:
-                row = piece(lanes + slots(here, rows, b, "row", t), 1)
-                phi.append(jnp.where(row_index == 0, row, piece((t * pair + b) * rows, rows)))
-    for b in range(pair):
-        phi.append(piece(lanes + (pair + b) * rows, rows))
-    for t in range(here):
-        for b in range(pair):
-            mine = phi[t * pair + b]
-            time_rate = phi[(t + 1) * pair + b] - mine
-            if t == here - 1:
-                time_rate = time_rate * inside
-            row = piece(lanes + slots(here, rows, b, "next", t), 1)
-            below = jnp.where(row_index == rows - 1, row, pltpu.roll(mine, rows - 1, 0))
-            gradient = (time_rate, below - mine, pltpu.roll(mine, cols - 1, 1) - mine)
-            mult = [mult_ref[c, t, q * pair + b] for c in range(3)]
-            time_part, one, two = (g + m for g, m in zip(gradient, mult))
-            kinetic = 0.5 * (one * one + two * two)
-            center = 1.0 + time_part
-            scaling = jnp.maximum(center, 1.0) + jnp.exp(jnp.log(kinetic) * (1.0 / 3.0))
-            twice = center + center
-            for _ in range(NEWTON):
-                residue = scaling * scaling * (scaling - center) - kinetic
-                derivative = scaling * (3.0 * scaling - twice)
-                change = residue * pl.reciprocal(derivative, approx=True)
-                scaling = jnp.maximum(scaling - change, 1.0)
-            feasible = time_part + kinetic <= 0.0
-            shrink = jnp.where(feasible, 1.0, 1.0 / scaling)
-            fresh = (
-                jnp.where(feasible, time_part, time_part - (scaling - 1.0)),
-                one * shrink,
-                two * shrink,
-            )
-            for c in range(3):
-                aux_out[c, t, q * pair + b] = fresh[c]
-                mult_out[c, t, q * pair + b] = mult[c] + (gradient[c] - fresh[c])
+    full = (pair, rows, cols)
+    row_index = lax.broadcasted_iota(jnp.int32, full, 1)
+    at = slice(q * pair, (q + 1) * pair)
+
+    def level(start):
+        return values[start : start + pair * rows].reshape(full)
+
+    def rims(kind, t):
+        starts = [lanes + slots(here, rows, b, kind, t) for b in range(pair)]
+        rim = [jnp.broadcast_to(values[start : start + 1], (rows, cols)) for start in starts]
+        return jnp.concatenate(rim, axis=0).reshape(full)
+
+    phi = [level(lanes)]
+    for t in range(1, here):
+        phi.append(jnp.where(row_index == 0, rims("row", t), level(t * pair * rows)))
+    phi.append(level(lanes + pair * rows))
+    for t0 in range(0, here, 1):
+        times = range(t0, t0 + 1)
+        mine = jnp.concatenate([phi[t] for t in times], axis=0)
+        rate = jnp.concatenate([phi[t + 1] for t in times], axis=0) - mine
+        if times[-1] == here - 1:
+            kept = [rate[: (1 - 1) * pair]] if 1 > 1 else []
+            rate = jnp.concatenate(kept + [rate[(1 - 1) * pair :] * inside], axis=0)
+        rim = jnp.concatenate([rims("next", t) for t in times], axis=0)
+        index = lax.broadcasted_iota(jnp.int32, mine.shape, 1)
+        below = jnp.where(index == rows - 1, rim, pltpu.roll(mine, rows - 1, 1))
+        gradient = (rate, below - mine, pltpu.roll(mine, cols - 1, 2) - mine)
+        target = [
+            gradient[c] + jnp.concatenate([mult_ref[c, t, at] for t in times], axis=0)
+            for c in range(3)
+        ]
+        time_part, one, two = target
+        kinetic = 0.5 * (one * one + two * two)
+        center = 1.0 + time_part
+        scaling = jnp.maximum(center, 1.0) + jnp.exp(jnp.log(kinetic) * (1.0 / 3.0))
+        for _ in range(NEWTON):
+            linear = scaling * (scaling - center)
+            residue = scaling * linear - kinetic
+            derivative = scaling * scaling + (linear + linear)
+            change = residue * pl.reciprocal(derivative, approx=True)
+            scaling = jnp.maximum(scaling - change, 1.0)
+        scaling = jnp.where(time_part + kinetic <= 0.0, 1.0, scaling)
+        shrink = pl.reciprocal(scaling, approx=True)
+        shrink = shrink * (2.0 - scaling * shrink)
+        shrink = shrink * (2.0 - scaling * shrink)
+        moved = scaling - 1.0
+        fresh = (time_part - moved, one * shrink, two * shrink)
+        for c, past in enumerate((moved, one - fresh[1], two - fresh[2])):
+            for n, t in enumerate(times):
+                part = slice(n * pair, (n + 1) * pair)
+                aux_out[c, t, at] = fresh[c][part]
+                mult_out[c, t, at] = past[part]
 
 
 def params(size=48):
     return pltpu.CompilerParams(vmem_limit_bytes=size * 1024 * 1024)
-
-
-def whole_block(array):
-    return pl.BlockSpec(array.shape, lambda p: (0,) * array.ndim)
 
 
 def local(multiplier, auxiliary, density_start, density_end):
@@ -545,25 +597,28 @@
     ones = constant_source(here, rows, time_blocks, row_blocks, both).astype(np.float32)
     factors = elimination_table(levels, row_count, cols, row_blocks, pieces, pair)
 
-    group = GROUP
-    five = pl.BlockSpec((3, here, pair * group, rows, cols), lambda p: (0, 0, p, 0, 0))
-    chunks = pl.BlockSpec((row_blocks, group, kinds, few, lanes), lambda p: (0, p, 0, 0, 0))
     away = pl.BlockSpec(memory_space=pltpu.HBM)
+    vmem = pl.BlockSpec(memory_space=pltpu.VMEM)
     chunked = jax.ShapeDtypeStruct((row_blocks, time_blocks, kinds, few, lanes), jnp.float32)
-    kept = pl.BlockSpec((group, cols, lanes), lambda p: (p, 0, 0))
+    inner_shape = (time_blocks, cols, lanes)
     edges, inner = pl.pallas_call(
         functools.partial(source_kernel, levels, pair),
-        grid=(time_blocks // group,),
-        in_specs=[five, five] + [away] * 6,
-        out_specs=[chunks, kept],
-        out_shape=[chunked, jax.ShapeDtypeStruct((time_blocks, cols, lanes), jnp.float32)],
+        in_specs=[away] * 8,
+        out_specs=[away] * 2,
+        out_shape=[chunked, jax.ShapeDtypeStruct(inner_shape, jnp.float32)],
         scratch_shapes=[
+            pltpu.VMEM(multiplier.shape, jnp.float32),
+            pltpu.VMEM(auxiliary.shape, jnp.float32),
             pltpu.VMEM((2,) + density_start.shape, jnp.float32),
             pltpu.VMEM(hart_there.shape, jnp.bfloat16),
             pltpu.VMEM(basis2.shape[1:], jnp.bfloat16),
             pltpu.VMEM(inverse.shape[1:], jnp.float32),
             pltpu.VMEM(to_edges.shape[1:], jnp.bfloat16),
+            pltpu.VMEM(chunked.shape, jnp.float32),
+            pltpu.VMEM(inner_shape, jnp.float32),
+            pltpu.SemaphoreType.DMA((2, PARTS)),
             pltpu.SemaphoreType.DMA((6,)),
+            pltpu.SemaphoreType.DMA((2, PARTS)),
         ],
         compiler_params=params(56),
         name="source",
@@ -573,7 +628,6 @@
         flat = value.reshape((row_blocks * time_blocks,) + value.shape[2:])
         return lax.all_to_all(flat, EVERY, 0, 0, tiled=True).reshape(value.shape)
 
-    vmem = pl.BlockSpec(memory_space=pltpu.VMEM)
     solved = pl.pallas_call(
         solve_kernel,
         in_specs=[vmem, vmem, vmem, vmem, pl.BlockSpec(memory_space=pl.ANY)],
@@ -593,10 +647,14 @@
     result = jax.ShapeDtypeStruct(multiplier.shape, jnp.float32)
     mult_next, aux_next = pl.pallas_call(
         functools.partial(step_kernel, levels, pair),
-        grid=(time_blocks // group,),
-        in_specs=[five, chunks, kept]
-        + [whole_block(a) for a in (hart_back, from_edges, inverse, basis3)],
-        out_specs=[five, five],
+        in_specs=[away] + [vmem] * 6,
+        out_specs=[away] * 2,
+        scratch_shapes=[
+            pltpu.VMEM(multiplier.shape, jnp.float32),
+            pltpu.VMEM(multiplier.shape, jnp.float32),
+            pltpu.VMEM(multiplier.shape, jnp.float32),
+            pltpu.SemaphoreType.DMA((3, time_blocks)),
+        ],
         out_shape=[result, result],
         compiler_params=params(),
         name="step",

time: 71.3 us -> 67 us (0.940)
  Pallas kernels: 24.1 us -> 19.7 us
    pallas_call x2, Pallas kernels: 19.1 us -> 14.7 us  [the longest x1 8.02 us: local(): pl.pallas_call(functools.partial(step_kernel, levels, pair), in_specs=[aw...]
where the time goes in v3:
time: 67 us; the launch traced here: 66.8 us
  blocking collectives  46.1 us (69%)
  Pallas kernels  19.7 us (29%)
  between operations  0.88 us (1%)
    all_to_all x2, blocking collectives, spread(): return lax.all_to_all(flat, EVERY, 0, 0, tiled=True).reshape(value.shape)  46.1 us
    pallas_call x1, Pallas kernels, local(): pl.pallas_call(functools.partial(step_kernel, levels, pair), in_specs=[aw...  8.02 us
    pallas_call x1, Pallas kernels, local(): pl.pallas_call(functools.partial(source_kernel, levels, pair), in_specs=[...  6.65 us
    pallas_call x1, Pallas kernels, local(): pl.pallas_call(solve_kernel, in_specs=[vmem, vmem, vmem, vmem, pl.BlockSp...  5.05 us

profile of v3, /device:TPU:1, one launch (start us, length us, event | category | flops | bytes accessed | tf_op | source)
XLA Modules:
  0.0 66.8 jit_solution(4658210604681543313)
XLA Ops:
  0.6 0.0 copy-start
  0.6 0.0 copy-start.5
  0.7 0.0 copy-start.6
  0.7 6.7 %source.1 = (f32[16,8,5,2,128]{4,3,2,1,0:T(2,128)}, f32[8,256,128]{2,1,0:T(8,128)}) custom-call(f32[3,4,16,16,256]{4,3,2,1,0:T(8,128)} %mult_in.1, f32[3,4,16,16,256]{4,3,2,1,0:T(8,128)} %aux_hbm.1, f32[16,16,256]{2,1,0:T(8,128)} %start_hbm.1, f32[16,16,256]{2,1,0:T(8,128)} %end_hbm.1, bf16[256,768]{1,0:T(8,128)(2,1)} %constant.20.clone.hart_hbm, ...), custom_call_target="tpu_custom_call" | custom-call | tf_op jit(solution)/shard_map/source/pallas_call | solution.py:604
  7.3 26.8 %all_to_all.10 = f32[128,5,2,128]{3,2,1,0:T(2,128)S(1)} all-to-all(f32[128,5,2,128]{3,2,1,0:T(2,128)} %bitcast.7), channel_id=1, replica_groups=mesh['grp'=2,'px'=8,'py'=8] {'grp','px','py'}, dimensions={0} | all-to-all | bytes 1310720 | tf_op jit(solution)/shard_map/all_to_all | solution.py:629
  34.1 0.0 copy-done
  34.1 0.0 copy-done.5
  34.1 0.0 copy-done.6
  34.1 0.0 copy-start.1
  34.1 0.0 copy-start.2
  34.1 0.0 copy-start.3
  34.1 0.0 copy-start.4
  34.1 5.0 %solve.1 = f32[16,8,5,2,128]{4,3,2,1,0:T(2,128)S(1)} custom-call(f32[16,8,5,2,128]{4,3,2,1,0:T(2,128)S(1)} %bitcast.4, bf16[768,256]{1,0:T(8,128)(2,1)S(1)} %copy-done.5, bf16[1536,256]{1,0:T(8,128)(2,1)S(1)} %copy-done, f32[32,256]{1,0:T(8,128)S(1)} %copy-done.6, f32[16,17,32,256]{3,2,1,0:T(8,128)} %constant.27.clone.table_ref), custom_call_target="tpu_custom_call" | custom-call | tf_op jit(solution)/shard_map/solve/pallas_call | solution.py:631
  39.2 19.3 %all_to_all.11 = f32[128,5,2,128]{3,2,1,0:T(2,128)S(1)} all-to-all(f32[128,5,2,128]{3,2,1,0:T(2,128)S(1)} %bitcast.5), channel_id=1, replica_groups=mesh['grp'=2,'px'=8,'py'=8] {'grp','px','py'}, dimensions={0} | all-to-all | bytes 1310720 | tf_op jit(solution)/shard_map/all_to_all | solution.py:629
  58.6 0.0 copy-done.1
  58.6 0.0 copy-done.2
  58.6 0.0 copy-done.3
  58.6 0.0 copy-done.4
  58.6 8.0 %step.1 = (f32[3,4,16,16,256]{4,3,2,1,0:T(8,128)}, f32[3,4,16,16,256]{4,3,2,1,0:T(8,128)}) custom-call(f32[3,4,16,16,256]{4,3,2,1,0:T(8,128)} %mult_in.1, f32[16,8,5,2,128]{4,3,2,1,0:T(2,128)S(1)} %bitcast.6, f32[8,256,128]{2,1,0:T(8,128)S(1)} %copy-done.1, bf16[1536,256]{1,0:T(8,128)(2,1)S(1)} %copy-done, bf16[2,512,256]{2,1,0:T(8,128)(2,1)S(1)} %copy-done.4, ...), custom_call_target="tpu_custom_call" | custom-call | tf_op jit(solution)/shard_map/step/pallas_call | solution.py:648
Async XLA Ops:
  0.6 33.5 %copy-start = (bf16[1536,256]{1,0:T(8,128)(2,1)S(1)}, bf16[1536,256]{1,0:T(8,128)(2,1)}, u32[]{:S(2)}) copy-start(bf16[1536,256]{1,0:T(8,128)(2,1)} %constant.25.clone.back_ref.hart_ref) | copy-start | bytes 2359300
  0.6 33.5 %copy-start.5 = (bf16[768,256]{1,0:T(8,128)(2,1)S(1)}, bf16[768,256]{1,0:T(8,128)(2,1)}, u32[]{:S(2)}) copy-start(bf16[768,256]{1,0:T(8,128)(2,1)} %constant.24.clone.hart_ref) | copy-start | bytes 1179652
  0.7 33.4 %copy-start.6 = (f32[32,256]{1,0:T(8,128)S(1)}, f32[32,256]{1,0:T(8,128)}, u32[]{:S(2)}) copy-start(f32[32,256]{1,0:T(8,128)} %constant.26.clone.ones_ref) | copy-start | bytes 98308
  34.1 24.5 %copy-start.1 = (f32[8,256,128]{2,1,0:T(8,128)S(1)}, f32[8,256,128]{2,1,0:T(8,128)}, u32[]{:S(2)}) copy-start(f32[8,256,128]{2,1,0:T(8,128)} %get-tuple-element.5.inner_ref) | copy-start | bytes 3145732
  34.1 24.4 %copy-start.2 = (f32[2,256,128]{2,1,0:T(8,128)S(1)}, f32[2,256,128]{2,1,0:T(8,128)}, u32[]{:S(2)}) copy-start(f32[2,256,128]{2,1,0:T(8,128)} %constant.22.clone.inverse_hbm.inverse_ref) | copy-start | bytes 786436
  34.1 24.4 %copy-start.3 = (bf16[2,512,256]{2,1,0:T(8,128)(2,1)S(1)}, bf16[2,512,256]{2,1,0:T(8,128)(2,1)}, u32[]{:S(2)}) copy-start(bf16[2,512,256]{2,1,0:T(8,128)(2,1)} %constant.29.clone.basis_ref) | copy-start | bytes 1572868
  34.1 24.4 %copy-start.4 = (bf16[2,512,256]{2,1,0:T(8,128)(2,1)S(1)}, bf16[2,512,256]{2,1,0:T(8,128)(2,1)}, u32[]{:S(2)}) copy-start(bf16[2,512,256]{2,1,0:T(8,128)(2,1)} %constant.28.clone.links_ref) | copy-start | bytes 1572868

commit v4 on v3

--- a/solution.py
+++ b/solution.py
@@ -10,8 +10,9 @@
 
 NEWTON = 4
 ROWS = ("grp", "px")
-EVERY = ("grp", "px", "py")
+EVERY = ("px", "grp", "py")
 PARTS = 2
+FETCHES = 4
 STEP_PARTS = 2
 VMEM_BYTES = 48 * 1024 * 1024
 DIRECT = ((1,), (0,))
@@ -219,8 +220,8 @@
     at_end = first + here == levels
     last = at_end.astype(jnp.int32)
     fields = []
-    for part in range(PARTS):
-        cut = pl.ds(part * batch // PARTS, batch // PARTS)
+    for part in range(FETCHES):
+        cut = pl.ds(part * batch // FETCHES, batch // FETCHES)
         fields.append(
             [
                 pltpu.make_async_copy(
@@ -237,21 +238,22 @@
     ]
     start_copy = pltpu.make_async_copy(start_hbm, density_ref.at[0], table_sems.at[4])
     end_copy = pltpu.make_async_copy(end_hbm, density_ref.at[1], table_sems.at[5])
-    for copy in fields[0] + tables + [start_copy, end_copy] + sum(fields[1:], []):
+    for copy in fields[0] + [start_copy, end_copy] + fields[1] + tables + sum(fields[2:], []):
         copy.start()
 
     row_index = lax.broadcasted_iota(jnp.int32, (rows, cols), 0)
     first_row = row_index == 0
     outs = []
     for part in range(PARTS):
-        for copy in fields[part]:
-            copy.wait()
-        if part == 0:
-            start_copy.wait()
-            end_copy.wait()
         mine = range(part * total_pairs // PARTS, (part + 1) * total_pairs // PARTS)
         field = []
         for q in mine:
+            if q * FETCHES % total_pairs == 0:
+                for copy in fields[q * FETCHES // total_pairs]:
+                    copy.wait()
+            if q == 0:
+                start_copy.wait()
+                end_copy.wait()
             blocks = []
             earlier = [0.0] * pair
             rims = jnp.zeros((rows, cols), jnp.float32)
@@ -305,7 +307,7 @@
 
 
 def solve_kernel(
-    in_ref, hart_ref, back_ref, ones_ref, table_ref, out_ref, field_ref, mean_ref, factor_ref, rim_ref, sem
+    groups, in_ref, hart_ref, back_ref, ones_ref, table_ref, out_ref, field_ref, mean_ref, factor_ref, rim_ref, sem
 ):
     row_blocks, time_blocks, kinds, few, lanes = in_ref.shape
     levels, high, cols = field_ref.shape
@@ -315,7 +317,7 @@
     tall = (kinds - 1) * few
     count = high // tall
     half = levels // 2
-    mine = lax.axis_index("grp") * lax.axis_size("px") + lax.axis_index("px")
+    mine = lax.axis_index("px") * lax.axis_size("grp") + lax.axis_index("grp")
     fetch = pltpu.make_async_copy(table_ref.at[mine], factor_ref, sem)
     fetch.start()
     stack = tall // few
@@ -333,12 +335,16 @@
     def offset(kind, t):
         return slots(here, rows, 0, kind, t) - 4 * rows
 
+    def place(g, j):
+        block = g * pieces + j
+        return block % (row_blocks // groups) * groups + block // (row_blocks // groups)
+
     def exchange(get):
-        groups = [
-            exchange_pieces([get(g * pieces + j) for j in range(pieces)], rows)
+        halves = [
+            exchange_pieces([get(place(g, j)) for j in range(pieces)], rows)
             for g in range(row_blocks // pieces)
         ]
-        return [jnp.concatenate([group[k] for group in groups], axis=1) for k in range(pieces)]
+        return [jnp.concatenate([one[k] for one in halves], axis=1) for k in range(pieces)]
 
     for h in range(time_blocks // stack):
         times = slice(h * stack, (h + 1) * stack)
@@ -438,7 +444,7 @@
         for g in range(row_blocks // pieces):
             cut = slice(g * lanes, (g + 1) * lanes)
             for j, value in enumerate(exchange_pieces([a[:, cut] for a in main], rows)):
-                out_ref[g * pieces + j, i, : kinds - 1] = value.reshape(kinds - 1, few, lanes)
+                out_ref[place(g, j), i, : kinds - 1] = value.reshape(kinds - 1, few, lanes)
         return tuple(first)
 
     carry = (blank,) * count
@@ -450,7 +456,7 @@
             cut = slice(g * lanes, (g + 1) * lanes)
             rims = exchange_pieces([rim_ref[h, j, 0, :, cut] for j in range(pieces)], rows)
             for j, value in enumerate(rims):
-                out_ref[g * pieces + j, times, kinds - 1] = value.reshape(stack, few, lanes)
+                out_ref[place(g, j), times, kinds - 1] = value.reshape(stack, few, lanes)
 
 
 def step_kernel(
@@ -616,7 +622,7 @@
             pltpu.VMEM(to_edges.shape[1:], jnp.bfloat16),
             pltpu.VMEM(chunked.shape, jnp.float32),
             pltpu.VMEM(inner_shape, jnp.float32),
-            pltpu.SemaphoreType.DMA((2, PARTS)),
+            pltpu.SemaphoreType.DMA((2, FETCHES)),
             pltpu.SemaphoreType.DMA((6,)),
             pltpu.SemaphoreType.DMA((2, PARTS)),
         ],
@@ -629,7 +635,7 @@
         return lax.all_to_all(flat, EVERY, 0, 0, tiled=True).reshape(value.shape)
 
     solved = pl.pallas_call(
-        solve_kernel,
+        functools.partial(solve_kernel, lax.axis_size("grp")),
         in_specs=[vmem, vmem, vmem, vmem, pl.BlockSpec(memory_space=pl.ANY)],
         out_specs=vmem,
         out_shape=chunked,

time: 67 us -> 66.6 us (level)
  no operation moved by 1% of the time
where the time goes in v4:
time: 66.6 us; the launch traced here: 66.4 us
  blocking collectives  45.7 us (69%)
  Pallas kernels  19.7 us (30%)
  between operations  0.88 us (1%)
    all_to_all x2, blocking collectives, spread(): return lax.all_to_all(flat, EVERY, 0, 0, tiled=True).reshape(value.shape)  45.7 us
    pallas_call x1, Pallas kernels, local(): pl.pallas_call(functools.partial(step_kernel, levels, pair), in_specs=[aw...  8.02 us
    pallas_call x1, Pallas kernels, local(): pl.pallas_call(functools.partial(source_kernel, levels, pair), in_specs=[...  6.63 us
    pallas_call x1, Pallas kernels, local(): pl.pallas_call(functools.partial(solve_kernel, lax.axis_size('grp')), in_...  5.04 us

profile of v4, /device:TPU:1, one launch (start us, length us, event | category | flops | bytes accessed | tf_op | source)
XLA Modules:
  0.0 66.4 jit_solution(11270515348733856440)
XLA Ops:
  0.6 0.0 copy-start
  0.6 0.0 copy-start.5
  0.7 0.0 copy-start.6
  0.7 6.6 %source.1 = (f32[16,8,5,2,128]{4,3,2,1,0:T(2,128)}, f32[8,256,128]{2,1,0:T(8,128)}) custom-call(f32[3,4,16,16,256]{4,3,2,1,0:T(8,128)} %mult_in.1, f32[3,4,16,16,256]{4,3,2,1,0:T(8,128)} %aux_hbm.1, f32[16,16,256]{2,1,0:T(8,128)} %start_hbm.1, f32[16,16,256]{2,1,0:T(8,128)} %end_hbm.1, bf16[256,768]{1,0:T(8,128)(2,1)} %constant.20.clone.hart_hbm, ...), custom_call_target="tpu_custom_call" | custom-call | tf_op jit(solution)/shard_map/source/pallas_call | solution.py:610
  7.3 26.9 %all_to_all.10 = f32[128,5,2,128]{3,2,1,0:T(2,128)S(1)} all-to-all(f32[128,5,2,128]{3,2,1,0:T(2,128)} %bitcast.7), channel_id=1, replica_groups=mesh['grp'=2,'px'=8,'py'=8] {'px','grp','py'}, dimensions={0} | all-to-all | bytes 1310720 | tf_op jit(solution)/shard_map/all_to_all | solution.py:635
  34.2 0.0 copy-done
  34.2 0.0 copy-done.5
  34.2 0.0 copy-done.6
  34.3 0.0 copy-start.1
  34.3 0.0 copy-start.2
  34.3 0.0 copy-start.3
  34.3 0.0 copy-start.4
  34.3 5.0 %solve.1 = f32[16,8,5,2,128]{4,3,2,1,0:T(2,128)S(1)} custom-call(f32[16,8,5,2,128]{4,3,2,1,0:T(2,128)S(1)} %bitcast.4, bf16[768,256]{1,0:T(8,128)(2,1)S(1)} %copy-done.5, bf16[1536,256]{1,0:T(8,128)(2,1)S(1)} %copy-done, f32[32,256]{1,0:T(8,128)S(1)} %copy-done.6, f32[16,17,32,256]{3,2,1,0:T(8,128)} %constant.27.clone.table_ref), custom_call_target="tpu_custom_call" | custom-call | tf_op jit(solution)/shard_map/solve/pallas_call | solution.py:637
  39.4 18.8 %all_to_all.11 = f32[128,5,2,128]{3,2,1,0:T(2,128)S(1)} all-to-all(f32[128,5,2,128]{3,2,1,0:T(2,128)S(1)} %bitcast.5), channel_id=1, replica_groups=mesh['grp'=2,'px'=8,'py'=8] {'px','grp','py'}, dimensions={0} | all-to-all | bytes 1310720 | tf_op jit(solution)/shard_map/all_to_all | solution.py:635
  58.2 0.0 copy-done.1
  58.2 0.0 copy-done.2
  58.2 0.0 copy-done.3
  58.2 0.0 copy-done.4
  58.2 8.0 %step.1 = (f32[3,4,16,16,256]{4,3,2,1,0:T(8,128)}, f32[3,4,16,16,256]{4,3,2,1,0:T(8,128)}) custom-call(f32[3,4,16,16,256]{4,3,2,1,0:T(8,128)} %mult_in.1, f32[16,8,5,2,128]{4,3,2,1,0:T(2,128)S(1)} %bitcast.6, f32[8,256,128]{2,1,0:T(8,128)S(1)} %copy-done.1, bf16[1536,256]{1,0:T(8,128)(2,1)S(1)} %copy-done, bf16[2,512,256]{2,1,0:T(8,128)(2,1)S(1)} %copy-done.4, ...), custom_call_target="tpu_custom_call" | custom-call | tf_op jit(solution)/shard_map/step/pallas_call | solution.py:654
Async XLA Ops:
  0.6 33.6 %copy-start = (bf16[1536,256]{1,0:T(8,128)(2,1)S(1)}, bf16[1536,256]{1,0:T(8,128)(2,1)}, u32[]{:S(2)}) copy-start(bf16[1536,256]{1,0:T(8,128)(2,1)} %constant.25.clone.back_ref.hart_ref) | copy-start | bytes 2359300
  0.6 33.6 %copy-start.5 = (bf16[768,256]{1,0:T(8,128)(2,1)S(1)}, bf16[768,256]{1,0:T(8,128)(2,1)}, u32[]{:S(2)}) copy-start(bf16[768,256]{1,0:T(8,128)(2,1)} %constant.24.clone.hart_ref) | copy-start | bytes 1179652
  0.7 33.6 %copy-start.6 = (f32[32,256]{1,0:T(8,128)S(1)}, f32[32,256]{1,0:T(8,128)}, u32[]{:S(2)}) copy-start(f32[32,256]{1,0:T(8,128)} %constant.26.clone.ones_ref) | copy-start | bytes 98308
  34.3 23.9 %copy-start.1 = (f32[8,256,128]{2,1,0:T(8,128)S(1)}, f32[8,256,128]{2,1,0:T(8,128)}, u32[]{:S(2)}) copy-start(f32[8,256,128]{2,1,0:T(8,128)} %get-tuple-element.5.inner_ref) | copy-start | bytes 3145732
  34.3 23.9 %copy-start.2 = (f32[2,256,128]{2,1,0:T(8,128)S(1)}, f32[2,256,128]{2,1,0:T(8,128)}, u32[]{:S(2)}) copy-start(f32[2,256,128]{2,1,0:T(8,128)} %constant.22.clone.inverse_hbm.inverse_ref) | copy-start | bytes 786436
  34.3 23.9 %copy-start.3 = (bf16[2,512,256]{2,1,0:T(8,128)(2,1)S(1)}, bf16[2,512,256]{2,1,0:T(8,128)(2,1)}, u32[]{:S(2)}) copy-start(bf16[2,512,256]{2,1,0:T(8,128)(2,1)} %constant.29.clone.basis_ref) | copy-start | bytes 1572868
  34.3 23.9 %copy-start.4 = (bf16[2,512,256]{2,1,0:T(8,128)(2,1)S(1)}, bf16[2,512,256]{2,1,0:T(8,128)(2,1)}, u32[]{:S(2)}) copy-start(bf16[2,512,256]{2,1,0:T(8,128)(2,1)} %constant.28.clone.links_ref) | copy-start | bytes 1572868

commit v5 on v4

--- a/solution.py
+++ b/solution.py
@@ -332,9 +332,6 @@
     def swap(value):
         return pltpu.roll(value, tall // 2, 0)
 
-    def offset(kind, t):
-        return slots(here, rows, 0, kind, t) - 4 * rows
-
     def place(g, j):
         block = g * pieces + j
         return block % (row_blocks // groups) * groups + block // (row_blocks // groups)
@@ -365,11 +362,9 @@
                 [rim_ref[i // stack, 2 * q + j, b, here_rows] for j in range(2) for b in range(2)],
                 axis=0,
             )
+            rim = jnp.where(lane < here - 1, rim, 0.0) + shift(rim, rows - here)
             for t in range(here):
-                value = shift(rim, rows - offset("next", t))
-                if t > 0:
-                    value = value + shift(rim, -offset("row", t))
-                value = jnp.where(lane == 0, value, 0.0)
+                value = jnp.where(lane == 0, rim if t == 1 else shift(rim, 1 - t), 0.0)
                 field[t].append(value + level if t == 0 else value)
         field = jnp.concatenate(sum(field, []), axis=0)
         modes = one_product(long_data(field, 2, 1), hart_ref[...], DIRECT)
@@ -427,13 +422,12 @@
         main, first = [], []
         for q in range(count):
             part = [values[t * high + q * tall : t * high + (q + 1) * tall] for t in range(here)]
-            rim = jnp.where(lane == offset("next", here), mean_ref[q], 0.0)
-            for t in range(here):
-                at = offset("next", t)
-                rim = jnp.where(lane == at, shift(part[t], at - rows), rim)
-                if t > 0:
-                    at = offset("row", t)
-                    rim = jnp.where(lane == at, shift(part[t], at), rim)
+            rim = jnp.where(lane == rows - 1, shift(part[0], -1), part[1])
+            for t in range(2, here):
+                rim = jnp.where(lane == t - 1, shift(part[t], t - 1), rim)
+            after = jnp.where(lane < 2 * here - 1, shift(rim, here - rows), mean_ref[q])
+            rim = jnp.where(lane < here - 1, rim, after)
+            rim = jnp.where(lane < 2 * here, rim, 0.0)
             rim = jnp.where(even, rim, shift(rim, rows // 2))
             rim = rim + pltpu.roll(rim, tall - few, 0)
             rim_ref[i // stack, 2 * q, 0, here_rows] = rim[:few]

time: 66.6 us -> 65.9 us (0.989)
  Pallas kernels: 19.7 us -> 19 us
where the time goes in v5:
time: 65.9 us; the launch traced here: 65.7 us
  blocking collectives  45.7 us (69%)
  Pallas kernels  19 us (29%)
  between operations  0.88 us (1%)
    all_to_all x2, blocking collectives, spread(): return lax.all_to_all(flat, EVERY, 0, 0, tiled=True).reshape(value.shape)  45.7 us
    pallas_call x1, Pallas kernels, local(): pl.pallas_call(functools.partial(step_kernel, levels, pair), in_specs=[aw...  8.02 us
    pallas_call x1, Pallas kernels, local(): pl.pallas_call(functools.partial(source_kernel, levels, pair), in_specs=[...  6.63 us
    pallas_call x1, Pallas kernels, local(): pl.pallas_call(functools.partial(solve_kernel, lax.axis_size('grp')), in_...  4.4 us

profile of v5, /device:TPU:1, one launch (start us, length us, event | category | flops | bytes accessed | tf_op | source)
XLA Modules:
  0.0 65.7 jit_solution(16375139499035592477)
XLA Ops:
  0.6 0.0 copy-start
  0.6 0.0 copy-start.5
  0.7 0.0 copy-start.6
  0.7 6.6 %source.1 = (f32[16,8,5,2,128]{4,3,2,1,0:T(2,128)}, f32[8,256,128]{2,1,0:T(8,128)}) custom-call(f32[3,4,16,16,256]{4,3,2,1,0:T(8,128)} %mult_in.1, f32[3,4,16,16,256]{4,3,2,1,0:T(8,128)} %aux_hbm.1, f32[16,16,256]{2,1,0:T(8,128)} %start_hbm.1, f32[16,16,256]{2,1,0:T(8,128)} %end_hbm.1, bf16[256,768]{1,0:T(8,128)(2,1)} %constant.20.clone.hart_hbm, ...), custom_call_target="tpu_custom_call" | custom-call | tf_op jit(solution)/shard_map/source/pallas_call | solution.py:604
  7.3 26.9 %all_to_all.10 = f32[128,5,2,128]{3,2,1,0:T(2,128)S(1)} all-to-all(f32[128,5,2,128]{3,2,1,0:T(2,128)} %bitcast.7), channel_id=1, replica_groups=mesh['grp'=2,'px'=8,'py'=8] {'px','grp','py'}, dimensions={0} | all-to-all | bytes 1310720 | tf_op jit(solution)/shard_map/all_to_all | solution.py:629
  34.2 0.0 copy-done
  34.2 0.0 copy-done.5
  34.2 0.0 copy-done.6
  34.3 0.0 copy-start.1
  34.3 0.0 copy-start.2
  34.3 0.0 copy-start.3
  34.3 0.0 copy-start.4
  34.3 4.4 %solve.1 = f32[16,8,5,2,128]{4,3,2,1,0:T(2,128)S(1)} custom-call(f32[16,8,5,2,128]{4,3,2,1,0:T(2,128)S(1)} %bitcast.4, bf16[768,256]{1,0:T(8,128)(2,1)S(1)} %copy-done.5, bf16[1536,256]{1,0:T(8,128)(2,1)S(1)} %copy-done, f32[32,256]{1,0:T(8,128)S(1)} %copy-done.6, f32[16,17,32,256]{3,2,1,0:T(8,128)} %constant.27.clone.table_ref), custom_call_target="tpu_custom_call" | custom-call | tf_op jit(solution)/shard_map/solve/pallas_call | solution.py:631
  38.7 18.8 %all_to_all.11 = f32[128,5,2,128]{3,2,1,0:T(2,128)S(1)} all-to-all(f32[128,5,2,128]{3,2,1,0:T(2,128)S(1)} %bitcast.5), channel_id=1, replica_groups=mesh['grp'=2,'px'=8,'py'=8] {'px','grp','py'}, dimensions={0} | all-to-all | bytes 1310720 | tf_op jit(solution)/shard_map/all_to_all | solution.py:629
  57.5 0.0 copy-done.1
  57.5 0.0 copy-done.2
  57.5 0.0 copy-done.3
  57.5 0.0 copy-done.4
  57.5 8.0 %step.1 = (f32[3,4,16,16,256]{4,3,2,1,0:T(8,128)}, f32[3,4,16,16,256]{4,3,2,1,0:T(8,128)}) custom-call(f32[3,4,16,16,256]{4,3,2,1,0:T(8,128)} %mult_in.1, f32[16,8,5,2,128]{4,3,2,1,0:T(2,128)S(1)} %bitcast.6, f32[8,256,128]{2,1,0:T(8,128)S(1)} %copy-done.1, bf16[1536,256]{1,0:T(8,128)(2,1)S(1)} %copy-done, bf16[2,512,256]{2,1,0:T(8,128)(2,1)S(1)} %copy-done.4, ...), custom_call_target="tpu_custom_call" | custom-call | tf_op jit(solution)/shard_map/step/pallas_call | solution.py:648
Async XLA Ops:
  0.6 33.6 %copy-start = (bf16[1536,256]{1,0:T(8,128)(2,1)S(1)}, bf16[1536,256]{1,0:T(8,128)(2,1)}, u32[]{:S(2)}) copy-start(bf16[1536,256]{1,0:T(8,128)(2,1)} %constant.25.clone.back_ref.hart_ref) | copy-start | bytes 2359300
  0.6 33.6 %copy-start.5 = (bf16[768,256]{1,0:T(8,128)(2,1)S(1)}, bf16[768,256]{1,0:T(8,128)(2,1)}, u32[]{:S(2)}) copy-start(bf16[768,256]{1,0:T(8,128)(2,1)} %constant.24.clone.hart_ref) | copy-start | bytes 1179652
  0.7 33.6 %copy-start.6 = (f32[32,256]{1,0:T(8,128)S(1)}, f32[32,256]{1,0:T(8,128)}, u32[]{:S(2)}) copy-start(f32[32,256]{1,0:T(8,128)} %constant.26.clone.ones_ref) | copy-start | bytes 98308
  34.3 23.3 %copy-start.1 = (f32[8,256,128]{2,1,0:T(8,128)S(1)}, f32[8,256,128]{2,1,0:T(8,128)}, u32[]{:S(2)}) copy-start(f32[8,256,128]{2,1,0:T(8,128)} %get-tuple-element.5.inner_ref) | copy-start | bytes 3145732
  34.3 23.3 %copy-start.2 = (f32[2,256,128]{2,1,0:T(8,128)S(1)}, f32[2,256,128]{2,1,0:T(8,128)}, u32[]{:S(2)}) copy-start(f32[2,256,128]{2,1,0:T(8,128)} %constant.22.clone.inverse_hbm.inverse_ref) | copy-start | bytes 786436
  34.3 23.3 %copy-start.3 = (bf16[2,512,256]{2,1,0:T(8,128)(2,1)S(1)}, bf16[2,512,256]{2,1,0:T(8,128)(2,1)}, u32[]{:S(2)}) copy-start(bf16[2,512,256]{2,1,0:T(8,128)(2,1)} %constant.29.clone.basis_ref) | copy-start | bytes 1572868
  34.3 23.3 %copy-start.4 = (bf16[2,512,256]{2,1,0:T(8,128)(2,1)S(1)}, bf16[2,512,256]{2,1,0:T(8,128)(2,1)}, u32[]{:S(2)}) copy-start(bf16[2,512,256]{2,1,0:T(8,128)(2,1)} %constant.28.clone.links_ref) | copy-start | bytes 1572868

commit v6 on v5

--- a/solution.py
+++ b/solution.py
@@ -195,8 +195,10 @@
     basis_hbm,
     inverse_hbm,
     edges_hbm,
+    factors_hbm,
     out_hbm,
     inner_hbm,
+    factor_hbm,
     mult_ref,
     aux_ref,
     density_ref,
@@ -236,14 +238,16 @@
         pltpu.make_async_copy(inverse_hbm.at[last], inverse_ref, table_sems.at[2]),
         pltpu.make_async_copy(edges_hbm.at[last], edges_ref, table_sems.at[3]),
     ]
+    modes_here = lax.axis_index("px") * lax.axis_size("grp") + lax.axis_index("grp")
+    factor_copy = pltpu.make_async_copy(factors_hbm.at[modes_here], factor_hbm, table_sems.at[6])
     start_copy = pltpu.make_async_copy(start_hbm, density_ref.at[0], table_sems.at[4])
     end_copy = pltpu.make_async_copy(end_hbm, density_ref.at[1], table_sems.at[5])
-    for copy in fields[0] + [start_copy, end_copy] + fields[1] + tables + sum(fields[2:], []):
+    for copy in fields[0] + [start_copy, end_copy] + fields[1] + tables + sum(fields[2:], []) + [factor_copy]:
         copy.start()
 
     row_index = lax.broadcasted_iota(jnp.int32, (rows, cols), 0)
     first_row = row_index == 0
-    outs = []
+    outs = [factor_copy]
     for part in range(PARTS):
         mine = range(part * total_pairs // PARTS, (part + 1) * total_pairs // PARTS)
         field = []
@@ -286,28 +290,28 @@
                 copy.wait()
         modes = [one_product(hart_ref[...], nodes, CROSS) for nodes in field]
         inner = [wide_product(mode[:, :lanes], basis_ref[...], 2) for mode in modes]
+        for n, q in enumerate(mine):
+            inner_ref[q] = inner[n]
+            outs.append(pltpu.make_async_copy(inner_ref.at[q], inner_hbm.at[q], out_sems.at[1, q]))
+            outs[-1].start()
         gone = [wide_product(value * inverse_ref[...], edges_ref[...], 2) for value in inner]
         for n, q in enumerate(mine):
-            inner_ref[q] = inner[n]
             edges = modes[n][:, lanes:] + gone[n]
             blocks = exchange_pieces(
                 [edges[j * each : (j + 1) * each] for j in range(pieces)], rows
             )
             for k in range(out_ref.shape[2]):
                 out_ref[:, q, k] = blocks[k].reshape(out_ref.shape[0], out_ref.shape[3], lanes)
-        cut = pl.ds(mine[0], len(mine))
-        outs += [
-            pltpu.make_async_copy(out_ref.at[:, cut], out_hbm.at[:, cut], out_sems.at[0, part]),
-            pltpu.make_async_copy(inner_ref.at[cut], inner_hbm.at[cut], out_sems.at[1, part]),
-        ]
-        for copy in outs[-2:]:
-            copy.start()
+            outs.append(
+                pltpu.make_async_copy(out_ref.at[:, q], out_hbm.at[:, q], out_sems.at[0, q])
+            )
+            outs[-1].start()
     for copy in outs:
         copy.wait()
 
 
 def solve_kernel(
-    groups, in_ref, hart_ref, back_ref, ones_ref, table_ref, out_ref, field_ref, mean_ref, factor_ref, rim_ref, sem
+    groups, in_ref, hart_ref, back_ref, ones_ref, factor_ref, out_ref, field_ref, mean_ref, rim_ref
 ):
     row_blocks, time_blocks, kinds, few, lanes = in_ref.shape
     levels, high, cols = field_ref.shape
@@ -318,8 +322,6 @@
     count = high // tall
     half = levels // 2
     mine = lax.axis_index("px") * lax.axis_size("grp") + lax.axis_index("grp")
-    fetch = pltpu.make_async_copy(table_ref.at[mine], factor_ref, sem)
-    fetch.start()
     stack = tall // few
     lane = lax.broadcasted_iota(jnp.int32, (tall, cols), 1) % rows
     row = lax.broadcasted_iota(jnp.int32, (tall, cols), 0)
@@ -375,7 +377,6 @@
     carry = (blank,) * count
     for i in range(time_blocks):
         carry = forward(i, carry)
-    fetch.wait()
 
     mean_ref[...] = jnp.zeros(mean_ref.shape, jnp.float32)
 
@@ -601,11 +602,15 @@
     vmem = pl.BlockSpec(memory_space=pltpu.VMEM)
     chunked = jax.ShapeDtypeStruct((row_blocks, time_blocks, kinds, few, lanes), jnp.float32)
     inner_shape = (time_blocks, cols, lanes)
-    edges, inner = pl.pallas_call(
+    edges, inner, factor = pl.pallas_call(
         functools.partial(source_kernel, levels, pair),
-        in_specs=[away] * 8,
-        out_specs=[away] * 2,
-        out_shape=[chunked, jax.ShapeDtypeStruct(inner_shape, jnp.float32)],
+        in_specs=[away] * 9,
+        out_specs=[away] * 3,
+        out_shape=[
+            chunked,
+            jax.ShapeDtypeStruct(inner_shape, jnp.float32),
+            jax.ShapeDtypeStruct(factors.shape[1:], jnp.float32),
+        ],
         scratch_shapes=[
             pltpu.VMEM(multiplier.shape, jnp.float32),
             pltpu.VMEM(auxiliary.shape, jnp.float32),
@@ -617,12 +622,12 @@
             pltpu.VMEM(chunked.shape, jnp.float32),
             pltpu.VMEM(inner_shape, jnp.float32),
             pltpu.SemaphoreType.DMA((2, FETCHES)),
-            pltpu.SemaphoreType.DMA((6,)),
-            pltpu.SemaphoreType.DMA((2, PARTS)),
+            pltpu.SemaphoreType.DMA((7,)),
+            pltpu.SemaphoreType.DMA((2, time_blocks)),
         ],
         compiler_params=params(56),
         name="source",
-    )(multiplier, auxiliary, density_start, density_end, hart_there, basis2, inverse, to_edges)
+    )(multiplier, auxiliary, density_start, density_end, hart_there, basis2, inverse, to_edges, factors)
 
     def spread(value):
         flat = value.reshape((row_blocks * time_blocks,) + value.shape[2:])
@@ -630,19 +635,17 @@
 
     solved = pl.pallas_call(
         functools.partial(solve_kernel, lax.axis_size("grp")),
-        in_specs=[vmem, vmem, vmem, vmem, pl.BlockSpec(memory_space=pl.ANY)],
+        in_specs=[vmem] * 5,
         out_specs=vmem,
         out_shape=chunked,
         scratch_shapes=[
             pltpu.VMEM((levels, pair * pieces * few, row_count), jnp.float32),
             pltpu.VMEM((pieces // 2, 2 * pair * few, row_count), jnp.float32),
-            pltpu.VMEM(factors.shape[1:], jnp.float32),
             pltpu.VMEM((time_blocks // (2 * pair), pieces, 2, 2 * pair * few, row_count), jnp.float32),
-            pltpu.SemaphoreType.DMA,
         ],
         compiler_params=params(),
         name="solve",
-    )(spread(edges), rows_there, rows_back, ones, factors)
+    )(spread(edges), rows_there, rows_back, ones, factor)
 
     result = jax.ShapeDtypeStruct(multiplier.shape, jnp.float32)
     mult_next, aux_next = pl.pallas_call(

time: 65.9 us -> 77.8 us (1.18)
  Pallas kernels: 19 us -> 29.8 us
  local copies, waits for them, and re-layouts: 0.05 us -> 1.09 us
    pallas_call x1, Pallas kernels: 6.63 us -> 18.3 us  [local(): pl.pallas_call(functools.partial(source_kernel, levels, pair), in_specs=[...]
    unnamed x14 -> x16, local copies, waits for them, and re-layouts: 0.05 us -> 1.09 us
    pallas_call x1, Pallas kernels: 4.4 us -> 3.45 us  [local(): pl.pallas_call(functools.partial(solve_kernel, lax.axis_size('grp')), in_...]
where the time goes in v6:
time: 77.8 us; the launch traced here: 77.5 us
  blocking collectives  45.8 us (59%)
  Pallas kernels  29.8 us (38%)
  local copies, waits for them, and re-layouts  1.09 us (1%)
  between operations  0.89 us (1%)
    all_to_all x2, blocking collectives, spread(): return lax.all_to_all(flat, EVERY, 0, 0, tiled=True).reshape(value.shape)  45.8 us
    pallas_call x1, Pallas kernels, local(): pl.pallas_call(functools.partial(source_kernel, levels, pair), in_specs=[...  18.3 us
    pallas_call x1, Pallas kernels, local(): pl.pallas_call(functools.partial(step_kernel, levels, pair), in_specs=[aw...  8.02 us
    pallas_call x1, Pallas kernels, local(): pl.pallas_call(functools.partial(solve_kernel, lax.axis_size('grp')), in_...  3.45 us

profile of v6, /device:TPU:1, one launch (start us, length us, event | category | flops | bytes accessed | tf_op | source)
XLA Modules:
  0.0 77.5 jit_solution(10619648923713819540)
XLA Ops:
  0.6 0.0 copy-start
  0.6 0.0 copy-start.6
  0.7 0.0 copy-start.7
  0.7 0.0 copy-start.4
  0.7 0.0 copy-start.5
  0.7 18.3 %source.1 = (f32[16,8,5,2,128]{4,3,2,1,0:T(2,128)}, f32[8,256,128]{2,1,0:T(8,128)}, f32[17,32,256]{2,1,0:T(8,128)}) custom-call(f32[3,4,16,16,256]{4,3,2,1,0:T(8,128)} %mult_in.1, f32[3,4,16,16,256]{4,3,2,1,0:T(8,128)} %aux_hbm.1, f32[16,16,256]{2,1,0:T(8,128)} %start_hbm.1, f32[16,16,256]{2,1,0:T(8,128)} %end_hbm.1, ...), custom_call_target="tpu_custom_call" | custom-call | tf_op jit(solution)/shard_map/source/pallas_call | solution.py:605
  19.0 0.0 copy-start.1
  19.0 0.0 copy-start.2
  19.0 26.9 %all_to_all.10 = f32[128,5,2,128]{3,2,1,0:T(2,128)S(1)} all-to-all(f32[128,5,2,128]{3,2,1,0:T(2,128)} %bitcast.7), channel_id=1, replica_groups=mesh['grp'=2,'px'=8,'py'=8] {'px','grp','py'}, dimensions={0} | all-to-all | bytes 1310720 | tf_op jit(solution)/shard_map/all_to_all | solution.py:634
  46.0 0.0 copy-done
  46.0 0.0 copy-done.6
  46.0 0.0 copy-done.7
  46.0 0.0 copy-start.3
  46.0 1.0 %copy-done.3 = f32[17,32,256]{2,1,0:T(8,128)S(1)} copy-done((f32[17,32,256]{2,1,0:T(8,128)S(1)}, f32[17,32,256]{2,1,0:T(8,128)}, u32[]{:S(2)}) %copy-start.3) | copy-done | bytes 557080
  47.0 3.5 %solve.1 = f32[16,8,5,2,128]{4,3,2,1,0:T(2,128)S(1)} custom-call(f32[16,8,5,2,128]{4,3,2,1,0:T(2,128)S(1)} %bitcast.4, bf16[768,256]{1,0:T(8,128)(2,1)S(1)} %copy-done.6, bf16[1536,256]{1,0:T(8,128)(2,1)S(1)} %copy-done, f32[32,256]{1,0:T(8,128)S(1)} %copy-done.7, f32[17,32,256]{2,1,0:T(8,128)S(1)} %copy-done.3), custom_call_target="tpu_custom_call" | custom-call | tf_op jit(solution)/shard_map/solve/pallas_call | solution.py:636
  50.5 18.8 %all_to_all.11 = f32[128,5,2,128]{3,2,1,0:T(2,128)S(1)} all-to-all(f32[128,5,2,128]{3,2,1,0:T(2,128)S(1)} %bitcast.5), channel_id=1, replica_groups=mesh['grp'=2,'px'=8,'py'=8] {'px','grp','py'}, dimensions={0} | all-to-all | bytes 1310720 | tf_op jit(solution)/shard_map/all_to_all | solution.py:634
  69.3 0.0 copy-done.4
  69.3 0.0 copy-done.5
  69.3 0.0 copy-done.1
  69.4 0.0 copy-done.2
  69.4 8.0 %step.1 = (f32[3,4,16,16,256]{4,3,2,1,0:T(8,128)}, f32[3,4,16,16,256]{4,3,2,1,0:T(8,128)}) custom-call(f32[3,4,16,16,256]{4,3,2,1,0:T(8,128)} %mult_in.1, f32[16,8,5,2,128]{4,3,2,1,0:T(2,128)S(1)} %bitcast.6, f32[8,256,128]{2,1,0:T(8,128)S(1)} %copy-done.2, bf16[1536,256]{1,0:T(8,128)(2,1)S(1)} %copy-done, bf16[2,512,256]{2,1,0:T(8,128)(2,1)S(1)} %copy-done.5, ...), custom_call_target="tpu_custom_call" | custom-call | tf_op jit(solution)/shard_map/step/pallas_call | solution.py:651
Async XLA Ops:
  0.6 45.3 %copy-start = (bf16[1536,256]{1,0:T(8,128)(2,1)S(1)}, bf16[1536,256]{1,0:T(8,128)(2,1)}, u32[]{:S(2)}) copy-start(bf16[1536,256]{1,0:T(8,128)(2,1)} %constant.26.clone.back_ref.hart_ref) | copy-start | bytes 2359300
  0.6 45.3 %copy-start.6 = (bf16[768,256]{1,0:T(8,128)(2,1)S(1)}, bf16[768,256]{1,0:T(8,128)(2,1)}, u32[]{:S(2)}) copy-start(bf16[768,256]{1,0:T(8,128)(2,1)} %constant.25.clone.hart_ref) | copy-start | bytes 1179652
  0.7 45.3 %copy-start.7 = (f32[32,256]{1,0:T(8,128)S(1)}, f32[32,256]{1,0:T(8,128)}, u32[]{:S(2)}) copy-start(f32[32,256]{1,0:T(8,128)} %constant.27.clone.ones_ref) | copy-start | bytes 98308
  0.7 68.7 %copy-start.4 = (bf16[2,512,256]{2,1,0:T(8,128)(2,1)S(1)}, bf16[2,512,256]{2,1,0:T(8,128)(2,1)}, u32[]{:S(2)}) copy-start(bf16[2,512,256]{2,1,0:T(8,128)(2,1)} %constant.29.clone.basis_ref) | copy-start | bytes 1572868
  0.7 68.7 %copy-start.5 = (bf16[2,512,256]{2,1,0:T(8,128)(2,1)S(1)}, bf16[2,512,256]{2,1,0:T(8,128)(2,1)}, u32[]{:S(2)}) copy-start(bf16[2,512,256]{2,1,0:T(8,128)(2,1)} %constant.28.clone.links_ref) | copy-start | bytes 1572868
  19.0 50.3 %copy-start.1 = (f32[2,256,128]{2,1,0:T(8,128)S(1)}, f32[2,256,128]{2,1,0:T(8,128)}, u32[]{:S(2)}) copy-start(f32[2,256,128]{2,1,0:T(8,128)} %constant.22.clone.inverse_hbm.inverse_ref) | copy-start | bytes 786436
  19.0 50.3 %copy-start.2 = (f32[8,256,128]{2,1,0:T(8,128)S(1)}, f32[8,256,128]{2,1,0:T(8,128)}, u32[]{:S(2)}) copy-start(f32[8,256,128]{2,1,0:T(8,128)} %get-tuple-element.7.inner_ref) | copy-start | bytes 3145732
  46.0 1.1 %copy-start.3 = (f32[17,32,256]{2,1,0:T(8,128)S(1)}, f32[17,32,256]{2,1,0:T(8,128)}, u32[]{:S(2)}) copy-start(f32[17,32,256]{2,1,0:T(8,128)} %get-tuple-element.6.factor_ref) | copy-start | bytes 1671172

commit v7 on v6

--- a/solution.py
+++ b/solution.py
@@ -206,6 +206,7 @@
     basis_ref,
     inverse_ref,
     edges_ref,
+    factor_ref,
     out_ref,
     inner_ref,
     field_sems,
@@ -239,7 +240,8 @@
         pltpu.make_async_copy(edges_hbm.at[last], edges_ref, table_sems.at[3]),
     ]
     modes_here = lax.axis_index("px") * lax.axis_size("grp") + lax.axis_index("grp")
-    factor_copy = pltpu.make_async_copy(factors_hbm.at[modes_here], factor_hbm, table_sems.at[6])
+    factor_copy = pltpu.make_async_copy(factors_hbm.at[modes_here], factor_ref, table_sems.at[6])
+    factor_out = pltpu.make_async_copy(factor_ref, factor_hbm, table_sems.at[7])
     start_copy = pltpu.make_async_copy(start_hbm, density_ref.at[0], table_sems.at[4])
     end_copy = pltpu.make_async_copy(end_hbm, density_ref.at[1], table_sems.at[5])
     for copy in fields[0] + [start_copy, end_copy] + fields[1] + tables + sum(fields[2:], []) + [factor_copy]:
@@ -247,7 +249,7 @@
 
     row_index = lax.broadcasted_iota(jnp.int32, (rows, cols), 0)
     first_row = row_index == 0
-    outs = [factor_copy]
+    outs = [factor_out]
     for part in range(PARTS):
         mine = range(part * total_pairs // PARTS, (part + 1) * total_pairs // PARTS)
         field = []
@@ -288,6 +290,9 @@
         if part == 0:
             for copy in tables:
                 copy.wait()
+        else:
+            factor_copy.wait()
+            factor_out.start()
         modes = [one_product(hart_ref[...], nodes, CROSS) for nodes in field]
         inner = [wide_product(mode[:, :lanes], basis_ref[...], 2) for mode in modes]
         for n, q in enumerate(mine):
@@ -619,10 +624,11 @@
             pltpu.VMEM(basis2.shape[1:], jnp.bfloat16),
             pltpu.VMEM(inverse.shape[1:], jnp.float32),
             pltpu.VMEM(to_edges.shape[1:], jnp.bfloat16),
+            pltpu.VMEM(factors.shape[1:], jnp.float32),
             pltpu.VMEM(chunked.shape, jnp.float32),
             pltpu.VMEM(inner_shape, jnp.float32),
             pltpu.SemaphoreType.DMA((2, FETCHES)),
-            pltpu.SemaphoreType.DMA((7,)),
+            pltpu.SemaphoreType.DMA((8,)),
             pltpu.SemaphoreType.DMA((2, time_blocks)),
         ],
         compiler_params=params(56),

time: 77.8 us -> 66 us (0.85)
  Pallas kernels: 29.8 us -> 18 us
    pallas_call x1, Pallas kernels: 18.3 us -> 6.53 us  [local(): pl.pallas_call(functools.partial(source_kernel, levels, pair), in_specs=[...]
where the time goes in v7:
time: 66 us; the launch traced here: 65.8 us
  blocking collectives  45.8 us (69%)
  Pallas kernels  18 us (27%)
  local copies, waits for them, and re-layouts  1.09 us (2%)
  between operations  0.89 us (1%)
    all_to_all x2, blocking collectives, spread(): return lax.all_to_all(flat, EVERY, 0, 0, tiled=True).reshape(value.shape)  45.8 us
    pallas_call x1, Pallas kernels, local(): pl.pallas_call(functools.partial(step_kernel, levels, pair), in_specs=[aw...  8.02 us
    pallas_call x1, Pallas kernels, local(): pl.pallas_call(functools.partial(source_kernel, levels, pair), in_specs=[...  6.53 us
    pallas_call x1, Pallas kernels, local(): pl.pallas_call(functools.partial(solve_kernel, lax.axis_size('grp')), in_...  3.46 us

profile of v7, /device:TPU:1, one launch (start us, length us, event | category | flops | bytes accessed | tf_op | source)
XLA Modules:
  0.0 65.8 jit_solution(18200822744646841932)
XLA Ops:
  0.6 0.0 copy-start
  0.6 0.0 copy-start.6
  0.7 0.0 copy-start.7
  0.7 0.0 copy-start.4
  0.7 0.0 copy-start.5
  0.7 6.5 %source.1 = (f32[16,8,5,2,128]{4,3,2,1,0:T(2,128)}, f32[8,256,128]{2,1,0:T(8,128)}, f32[17,32,256]{2,1,0:T(8,128)}) custom-call(f32[3,4,16,16,256]{4,3,2,1,0:T(8,128)} %mult_in.1, f32[3,4,16,16,256]{4,3,2,1,0:T(8,128)} %aux_hbm.1, f32[16,16,256]{2,1,0:T(8,128)} %start_hbm.1, f32[16,16,256]{2,1,0:T(8,128)} %end_hbm.1, ...), custom_call_target="tpu_custom_call" | custom-call | tf_op jit(solution)/shard_map/source/pallas_call | solution.py:610
  7.2 0.0 copy-start.1
  7.2 0.0 copy-start.2
  7.3 27.0 %all_to_all.10 = f32[128,5,2,128]{3,2,1,0:T(2,128)S(1)} all-to-all(f32[128,5,2,128]{3,2,1,0:T(2,128)} %bitcast.7), channel_id=1, replica_groups=mesh['grp'=2,'px'=8,'py'=8] {'px','grp','py'}, dimensions={0} | all-to-all | bytes 1310720 | tf_op jit(solution)/shard_map/all_to_all | solution.py:640
  34.2 0.0 copy-done
  34.2 0.0 copy-done.6
  34.2 0.0 copy-done.7
  34.2 0.0 copy-start.3
  34.2 1.0 %copy-done.3 = f32[17,32,256]{2,1,0:T(8,128)S(1)} copy-done((f32[17,32,256]{2,1,0:T(8,128)S(1)}, f32[17,32,256]{2,1,0:T(8,128)}, u32[]{:S(2)}) %copy-start.3) | copy-done | bytes 557080
  35.3 3.5 %solve.1 = f32[16,8,5,2,128]{4,3,2,1,0:T(2,128)S(1)} custom-call(f32[16,8,5,2,128]{4,3,2,1,0:T(2,128)S(1)} %bitcast.4, bf16[768,256]{1,0:T(8,128)(2,1)S(1)} %copy-done.6, bf16[1536,256]{1,0:T(8,128)(2,1)S(1)} %copy-done, f32[32,256]{1,0:T(8,128)S(1)} %copy-done.7, f32[17,32,256]{2,1,0:T(8,128)S(1)} %copy-done.3), custom_call_target="tpu_custom_call" | custom-call | tf_op jit(solution)/shard_map/solve/pallas_call | solution.py:642
  38.7 18.8 %all_to_all.11 = f32[128,5,2,128]{3,2,1,0:T(2,128)S(1)} all-to-all(f32[128,5,2,128]{3,2,1,0:T(2,128)S(1)} %bitcast.5), channel_id=1, replica_groups=mesh['grp'=2,'px'=8,'py'=8] {'px','grp','py'}, dimensions={0} | all-to-all | bytes 1310720 | tf_op jit(solution)/shard_map/all_to_all | solution.py:640
  57.6 0.0 copy-done.4
  57.6 0.0 copy-done.5
  57.6 0.0 copy-done.1
  57.6 0.0 copy-done.2
  57.6 8.0 %step.1 = (f32[3,4,16,16,256]{4,3,2,1,0:T(8,128)}, f32[3,4,16,16,256]{4,3,2,1,0:T(8,128)}) custom-call(f32[3,4,16,16,256]{4,3,2,1,0:T(8,128)} %mult_in.1, f32[16,8,5,2,128]{4,3,2,1,0:T(2,128)S(1)} %bitcast.6, f32[8,256,128]{2,1,0:T(8,128)S(1)} %copy-done.2, bf16[1536,256]{1,0:T(8,128)(2,1)S(1)} %copy-done, bf16[2,512,256]{2,1,0:T(8,128)(2,1)S(1)} %copy-done.5, ...), custom_call_target="tpu_custom_call" | custom-call | tf_op jit(solution)/shard_map/step/pallas_call | solution.py:657
Async XLA Ops:
  0.6 33.6 %copy-start = (bf16[1536,256]{1,0:T(8,128)(2,1)S(1)}, bf16[1536,256]{1,0:T(8,128)(2,1)}, u32[]{:S(2)}) copy-start(bf16[1536,256]{1,0:T(8,128)(2,1)} %constant.26.clone.back_ref.hart_ref) | copy-start | bytes 2359300
  0.6 33.6 %copy-start.6 = (bf16[768,256]{1,0:T(8,128)(2,1)S(1)}, bf16[768,256]{1,0:T(8,128)(2,1)}, u32[]{:S(2)}) copy-start(bf16[768,256]{1,0:T(8,128)(2,1)} %constant.25.clone.hart_ref) | copy-start | bytes 1179652
  0.7 33.6 %copy-start.7 = (f32[32,256]{1,0:T(8,128)S(1)}, f32[32,256]{1,0:T(8,128)}, u32[]{:S(2)}) copy-start(f32[32,256]{1,0:T(8,128)} %constant.27.clone.ones_ref) | copy-start | bytes 98308
  0.7 56.9 %copy-start.4 = (bf16[2,512,256]{2,1,0:T(8,128)(2,1)S(1)}, bf16[2,512,256]{2,1,0:T(8,128)(2,1)}, u32[]{:S(2)}) copy-start(bf16[2,512,256]{2,1,0:T(8,128)(2,1)} %constant.29.clone.basis_ref) | copy-start | bytes 1572868
  0.7 56.9 %copy-start.5 = (bf16[2,512,256]{2,1,0:T(8,128)(2,1)S(1)}, bf16[2,512,256]{2,1,0:T(8,128)(2,1)}, u32[]{:S(2)}) copy-start(bf16[2,512,256]{2,1,0:T(8,128)(2,1)} %constant.28.clone.links_ref) | copy-start | bytes 1572868
  7.2 50.3 %copy-start.1 = (f32[2,256,128]{2,1,0:T(8,128)S(1)}, f32[2,256,128]{2,1,0:T(8,128)}, u32[]{:S(2)}) copy-start(f32[2,256,128]{2,1,0:T(8,128)} %constant.22.clone.inverse_hbm.inverse_ref) | copy-start | bytes 786436
  7.2 50.3 %copy-start.2 = (f32[8,256,128]{2,1,0:T(8,128)S(1)}, f32[8,256,128]{2,1,0:T(8,128)}, u32[]{:S(2)}) copy-start(f32[8,256,128]{2,1,0:T(8,128)} %get-tuple-element.7.inner_ref) | copy-start | bytes 3145732
  34.2 1.1 %copy-start.3 = (f32[17,32,256]{2,1,0:T(8,128)S(1)}, f32[17,32,256]{2,1,0:T(8,128)}, u32[]{:S(2)}) copy-start(f32[17,32,256]{2,1,0:T(8,128)} %get-tuple-element.6.factor_ref) | copy-start | bytes 1671172
